TPU v7x, 512 devices: a whole 4x8x8 slice. The times are simulated.
512 devices in a mesh: dp: 64 (over x, z, core), tensor: 8 (over y).
Axes of the slice: x: 4, y: 8, z: 8, core: 2. Of those that a mesh axis runs over, the one named last changes fastest.
Arguments:
- prompt_keys: bfloat16 [4096, 1024], P('dp', 'tensor'), may hold values from -6 to 6
- prompt_values: bfloat16 [4096, 1024], P('dp', 'tensor'), may hold values from -6 to 6
- key_weight: bfloat16 [5120, 1024], P('dp', 'tensor'), may hold values from -0.078125 to 0.078125
- value_weight: bfloat16 [5120, 1024], P('dp', 'tensor'), may hold values from -0.078125 to 0.078125
- resp_query: bfloat16 [8192, 8192], P('dp', 'tensor'), may hold values from -6 to 6
- resp_keys: bfloat16 [8192, 1024], P('dp', 'tensor'), may hold values from -6 to 6
- resp_values: bfloat16 [8192, 1024], P('dp', 'tensor'), may hold values from -6 to 6
- resp_grad: bfloat16 [8192, 8192], P('dp', 'tensor'), may hold values from -48 to 48
- resp_lse: float32 [64, 8192], P('tensor', 'dp'), as said below
- resp_delta: float32 [64, 8192], P('tensor', 'dp'), may hold values from -24 to 24
- resp_prompt: int32 [1024], replicated, may hold values from 0 to 63, as said below
- resp_lengths: int32 [1024], P('dp'), may hold values from 1 to 8, 5120 in all
Outputs:
- d_query: bfloat16 [8192, 8192], P('dp', 'tensor')
- d_resp_keys: bfloat16 [8192, 1024], P('dp', 'tensor')
- d_resp_values: bfloat16 [8192, 1024], P('dp', 'tensor')
- d_prompt_input: bfloat16 [4096, 5120], P('dp', 'tensor')
Inputs may be any that keep to these rules, and one draw needn't show every extreme that they name: `resp_prompt`: response r sits on index r // 16 of dp, in slot r % 16, and prompt p on index p. For each slot number s, the responses in slot s of all indices of dp name every prompt exactly once; so each prompt is named by exactly 16 responses, and the 16 responses of one index of dp name 16 different prompts. `resp_lse`: within 0.5 below and 1.5 above log(72).
All inputs are finite; a program needn't handle non-finite values. No bound on the sum of `resp_lengths` on one device may be relied on, other than what follows from the above.
Results may differ from a plain program's by a relative error of at most 0.006.
Values may be sent and summed in bfloat16 or wider, within the bound.
A program may use at most 64 MiB of HBM per device.

v0:
```python
import jax
import jax.numpy as jnp
from jax import lax
from jax.sharding import PartitionSpec as P

QH = 64
KVH = 8
HD = 128


def attend_back(query, grad_live, log_norm, row_delta, key_rows, value_rows, key_mask):
    scaling = query.shape[-1] ** (-0.5)
    scores = (
        jnp.einsum("crlgqd,cmgd->crlgqm", query, key_rows, preferred_element_type=jnp.float32)
        * scaling
    )
    probs = jnp.exp(scores - log_norm[..., None])
    if key_mask is not None:
        probs = jnp.where(key_mask[:, None, None, :], probs, jnp.float32(0.0))
    probs_low = probs.astype(jnp.bfloat16)
    dprob = jnp.einsum(
        "crlgqd,cmgd->crlgqm", grad_live, value_rows, preferred_element_type=jnp.float32
    )
    dscore = (probs * (dprob - row_delta[..., None])).astype(jnp.bfloat16)
    grad_values = jnp.einsum(
        "crlgqm,crlgqd->cmgd", probs_low, grad_live, preferred_element_type=jnp.float32
    )
    grad_keys = (
        jnp.einsum("crlgqm,crlgqd->cmgd", dscore, query, preferred_element_type=jnp.float32)
        * scaling
    )
    grad_query = (
        jnp.einsum("crlgqm,cmgd->crlgqd", dscore, key_rows, preferred_element_type=jnp.float32)
        * scaling
    )
    return (grad_query, grad_keys, grad_values)


def prefix_scan(items, own_keys, own_values, group_size):
    count = items[0].shape[0]
    blocks = tuple(
        (
            part_array.reshape((count // group_size, group_size) + part_array.shape[1:])
            for part_array in items
        )
    )
    kv_local = own_keys.shape[2]
    head_size = own_keys.shape[3]

    def one_block(carry, block):
        got_query, got_grad, got_norm, got_delta = block
        rows_n, rows_l = (got_query.shape[0], got_query.shape[1])
        shaped_query = got_query.reshape(1, rows_n, rows_l, kv_local, -1, head_size)
        shaped_grad = got_grad.reshape(1, rows_n, rows_l, kv_local, -1, head_size)
        grad_query, grad_keys, grad_values = attend_back(
            shaped_query, shaped_grad, got_norm[None], got_delta[None], own_keys, own_values, None
        )
        return (
            (carry[0] + grad_keys, carry[1] + grad_values),
            grad_query.reshape(rows_n, rows_l, -1),
        )

    start_sums = (jnp.zeros(own_keys.shape, jnp.float32), jnp.zeros(own_keys.shape, jnp.float32))
    (key_sum, value_sum), block_dq = lax.scan(one_block, start_sums, blocks)
    return (key_sum, value_sum, block_dq.reshape((count,) + block_dq.shape[2:]))


def contract(left, right):
    return lax.dot_general(
        left, right, (((1,), (1,)), ((), ())), preferred_element_type=jnp.float32
    )


def body(
    prompt_keys,
    prompt_values,
    key_weight,
    value_weight,
    resp_query,
    resp_keys,
    resp_values,
    resp_grad,
    resp_lse,
    resp_delta,
    resp_prompt,
    resp_lengths,
):
    dev_count = lax.axis_size("dp")
    my_index = lax.axis_index("dp")
    group_heads = QH // KVH
    kv_local = resp_keys.shape[1] // HD
    slots = resp_lengths.shape[0]
    resp_len = resp_query.shape[0] // slots
    prompt_len = prompt_keys.shape[0]
    feat_width = resp_query.shape[1]
    zero_low = jnp.zeros((), jnp.bfloat16)
    shaped = (slots, resp_len, kv_local, group_heads, HD)
    valid = jnp.arange(resp_len)[None, :] < resp_lengths[:, None]
    query = resp_query.reshape(shaped)
    grad_live = jnp.where(valid[:, :, None, None, None], resp_grad.reshape(shaped), zero_low)
    log_norm = resp_lse.reshape(kv_local, group_heads, slots, resp_len).transpose(2, 3, 0, 1)
    delta_all = resp_delta.reshape(kv_local, group_heads, slots, resp_len).transpose(2, 3, 0, 1)
    delta_live = jnp.where(valid[:, :, None, None], delta_all, jnp.float32(0.0))
    placed = resp_prompt.reshape(dev_count, slots)
    my_prompts = lax.dynamic_slice_in_dim(placed, my_index, 1, 0)[0]
    flat_query = resp_query.reshape(slots, resp_len, feat_width)
    flat_grad = grad_live.reshape(slots, resp_len, feat_width)
    causal = jnp.arange(resp_len)[:, None] >= jnp.arange(resp_len)[None, :]
    key_local = resp_keys.reshape(slots, resp_len, kv_local, HD)
    value_local = resp_values.reshape(slots, resp_len, kv_local, HD)
    local_dq, local_dk, local_dv = attend_back(
        query[:, None],
        grad_live[:, None],
        log_norm[:, None],
        delta_live[:, None],
        key_local,
        value_local,
        causal,
    )
    d_resp_keys = local_dk.astype(jnp.bfloat16).reshape(slots * resp_len, kv_local * HD)
    d_resp_values = local_dv.astype(jnp.bfloat16).reshape(slots * resp_len, kv_local * HD)
    own_keys = prompt_keys.reshape(1, prompt_len, kv_local, HD)
    own_values = prompt_values.reshape(1, prompt_len, kv_local, HD)
    match = my_prompts[None, :] == jnp.arange(dev_count)[:, None]
    present = jnp.any(match, axis=1)
    dest_slot = jnp.sum(jnp.where(match, jnp.arange(slots)[None, :], 0), axis=1)
    send_query = jnp.where(
        present[:, None, None], jnp.take(flat_query, dest_slot, axis=0), zero_low
    )
    send_grad = jnp.where(present[:, None, None], jnp.take(flat_grad, dest_slot, axis=0), zero_low)
    send_norm = jnp.where(
        present[:, None, None, None], jnp.take(log_norm, dest_slot, axis=0), jnp.float32(0.0)
    )
    send_delta = jnp.where(
        present[:, None, None, None], jnp.take(delta_live, dest_slot, axis=0), jnp.float32(0.0)
    )
    send_query, send_grad, send_norm, send_delta = (send_query, send_grad, send_norm, send_delta)
    got_query, got_grad = (
        lax.all_to_all(send_query, "dp", split_axis=0, concat_axis=0, tiled=True),
        lax.all_to_all(send_grad, "dp", split_axis=0, concat_axis=0, tiled=True),
    )
    got_norm, got_delta = (
        lax.all_to_all(send_norm, "dp", split_axis=0, concat_axis=0, tiled=True),
        lax.all_to_all(send_delta, "dp", split_axis=0, concat_axis=0, tiled=True),
    )
    key_sum, value_sum, block_dq = prefix_scan(
        (got_query, got_grad, got_norm, got_delta), own_keys, own_values, slots
    )
    prefix_dq = block_dq.astype(jnp.bfloat16)
    returned = lax.all_to_all(prefix_dq, "dp", split_axis=0, concat_axis=0, tiled=True)
    mine = jnp.take(returned, my_prompts, axis=0)
    d_query = (local_dq.reshape(slots, resp_len, feat_width) + mine.astype(jnp.float32)).astype(
        jnp.bfloat16
    )
    d_query = d_query.reshape(slots * resp_len, feat_width)
    dk_low = key_sum.reshape(prompt_len, kv_local * HD).astype(jnp.bfloat16)
    dv_low = value_sum.reshape(prompt_len, kv_local * HD).astype(jnp.bfloat16)
    stacked = jnp.stack((key_weight, value_weight))
    piece = lax.all_gather(stacked, "dp", axis=1, tiled=True)
    partial_sum = contract(dk_low, piece[0]) + contract(dv_low, piece[1])
    summed = lax.psum_scatter(partial_sum, "tensor", scatter_dimension=1, tiled=True)
    d_prompt_input = summed.astype(jnp.bfloat16)
    return (d_query, d_resp_keys, d_resp_values, d_prompt_input)


def solution(mesh):
    placed = (
        P("dp", "tensor"),
        P("dp", "tensor"),
        P("dp", "tensor"),
        P("dp", "tensor"),
        P("dp", "tensor"),
        P("dp", "tensor"),
        P("dp", "tensor"),
        P("dp", "tensor"),
        P("tensor", "dp"),
        P("tensor", "dp"),
        P(),
        P("dp"),
    )
    return jax.shard_map(
        body,
        mesh=mesh,
        in_specs=placed,
        out_specs=(P("dp", "tensor"), P("dp", "tensor"), P("dp", "tensor"), P("dp", "tensor")),
        check_vma=False,
    )
```

profile of v0, /device:TPU:2, one launch (start us, length us, event | category | flops | bytes accessed | tf_op | source)
XLA Modules:
  0.0 240.0 jit_solution(2691822412907780129)
XLA Ops:
  7.2 0.8 reshape.275
  8.2 0.4 copy-done.7
  8.6 0.8 copy.93
  9.4 0.8 copy.94
  10.2 0.7 iota_compare_fusion.1
  11.0 0.6 gather_fusion.4
  11.7 0.6 gather_fusion.2
  12.3 1.0 fusion.39
  13.3 13.9 %all-to-all-start.1 = ((f32[64,8,1,8]{3,1,2,0:T(8,128)}), f32[64,8,1,8]{3,1,2,0:T(8,128)S(1)}, u32[]{:S(2)}, u32[]{:S(2)}) async-start(f32[64,8,1,8]{3,1,2,0:T(8,128)} %get-tuple-element.163), calls=%async_computation.1 | async-start | bytes 524288 | tf_op jit(solution)/shard_map/all_to_all | solution.py:143
  27.3 0.6 gather_fusion.3
  27.9 0.6 gather_fusion.1
  28.5 10.2 %all-to-all-done.1 = f32[64,8,1,8]{3,1,2,0:T(8,128)S(1)} async-done(((f32[64,8,1,8]{3,1,2,0:T(8,128)}), f32[64,8,1,8]{3,1,2,0:T(8,128)S(1)}, u32[]{:S(2)}, u32[]{:S(2)}) %all-to-all-start.1) | async-done | bytes 16416 | tf_op jit(solution)/shard_map/all_to_all | solution.py:143
  38.7 0.7 copy-done.4
  39.4 6.7 %all-to-all-start.3 = ((f32[64,8,1,8]{3,1,2,0:T(8,128)}), f32[64,8,1,8]{3,1,2,0:T(8,128)}, u32[]{:S(2)}, u32[]{:S(2)}) async-start(f32[64,8,1,8]{3,1,2,0:T(8,128)} %get-tuple-element.162), calls=%async_computation.3 | async-start | bytes 524288 | tf_op jit(solution)/shard_map/all_to_all | solution.py:144
  46.1 1.3 select_select_fusion
  47.4 10.1 %all-to-all-done.3 = f32[64,8,1,8]{3,1,2,0:T(8,128)} async-done(((f32[64,8,1,8]{3,1,2,0:T(8,128)}), f32[64,8,1,8]{3,1,2,0:T(8,128)}, u32[]{:S(2)}, u32[]{:S(2)}) %all-to-all-start.3) | async-done | bytes 16416 | tf_op jit(solution)/shard_map/all_to_all | solution.py:144
  57.5 33.4 %all_to_all.25 = bf16[64,8,1024]{2,1,0:T(8,128)(2,1)S(1)} all-to-all(bf16[64,8,1024]{2,1,0:T(8,128)(2,1)S(1)} %get-tuple-element.165), channel_id=1, replica_groups=mesh['dp'=64,'tensor'=8] {'dp'}, dimensions={0} | all-to-all | bytes 2097152 | tf_op jit(solution)/shard_map/all_to_all | solution.py:139
  91.0 8.0 %all-to-all-start.2 = ((bf16[64,8,1024]{2,1,0:T(8,128)(2,1)}), bf16[64,8,1024]{2,1,0:T(8,128)(2,1)}, u32[]{:S(2)}, u32[]{:S(2)}) async-start(bf16[64,8,1024]{2,1,0:T(8,128)(2,1)} %get-tuple-element.164), calls=%async_computation.2 | async-start | bytes 2097152 | tf_op jit(solution)/shard_map/all_to_all | solution.py:140
  99.0 0.6 pad_maximum_fusion
  99.7 26.2 %all-to-all-done.2 = bf16[64,8,1024]{2,1,0:T(8,128)(2,1)} async-done(((bf16[64,8,1024]{2,1,0:T(8,128)(2,1)}), bf16[64,8,1024]{2,1,0:T(8,128)(2,1)}, u32[]{:S(2)}, u32[]{:S(2)}) %all-to-all-start.2) | async-done | bytes 1048608 | tf_op jit(solution)/shard_map/all_to_all | solution.py:140
  126.0 15.7 %while.15 = (s32[]{:T(128)}, f32[1,64,1,128]{3,1,2,0:T(8,128)S(1)}, f32[1,64,1,128]{3,1,2,0:T(8,128)S(1)}, bf16[4,16,8,1024]{3,2,1,0:T(8,128)(2,1)}, bf16[4,16,8...) while((s32[]{:T(128)}, f32[1,64,1,128]{3,1,2,0:T(8,128)S(1)}, ...), condition=%wide.region_3.6_spmd.clone, body=%wide.region_2.5_spmd.clone.sunk | while | flops 84582400 | bytes 4792468 | solution.py:64
  126.0 0.9 dynamic-slice_bitcast_fusion.6
  126.8 1.0 dynamic-slice_bitcast_fusion.7
  127.8 0.2 fusion.85
  128.1 0.2 fusion.86
  128.3 0.2 fusion.87
  128.6 0.2 fusion.88
  129.2 0.7 constant_dynamic-update-slice_fusion.2
  129.9 0.9 dynamic-slice_bitcast_fusion.6
  130.8 1.0 dynamic-slice_bitcast_fusion.7
  131.8 0.2 fusion.85
  132.0 0.2 fusion.86
  132.3 0.2 fusion.87
  132.5 0.2 fusion.88
  133.1 0.7 constant_dynamic-update-slice_fusion.2
  133.8 0.9 dynamic-slice_bitcast_fusion.6
  134.7 1.0 dynamic-slice_bitcast_fusion.7
  135.7 0.2 fusion.85
  136.0 0.2 fusion.86
  136.2 0.2 fusion.87
  136.5 0.2 fusion.88
  137.0 0.7 constant_dynamic-update-slice_fusion.2
  137.8 0.9 dynamic-slice_bitcast_fusion.6
  138.7 1.0 dynamic-slice_bitcast_fusion.7
  139.6 0.2 fusion.85
  139.9 0.2 fusion.86
  140.2 0.2 fusion.87
  140.4 0.2 fusion.88
  141.0 0.7 constant_dynamic-update-slice_fusion.2
  141.7 46.2 %all-gather.2.cloned.1.call-done = bf16[2,5120,128]{2,1,0:T(8,128)(2,1)} async-done(((bf16[2,80,128]{2,1,0:T(8,128)(2,1)}), bf16[2,5120,128]{2,1,0:T(8,128)(2,1)}) %all-gather.2.cloned.1.call-update) | async-done | bytes 2621456 | tf_op jit(solution)/shard_map/all_gather | solution.py:159
  187.9 2.0 fusion.19
  190.1 1.6 convolution_add_fusion
  191.8 7.6 %all-to-all-start.4 = ((bf16[64,8,1024]{2,1,0:T(8,128)(2,1)}), bf16[64,8,1024]{2,1,0:T(8,128)(2,1)S(1)}, u32[]{:S(2)}, u32[]{:S(2)}) async-start(bf16[64,8,1024]{2,1,0:T(8,128)(2,1)} %bitcast.41), calls=%async_computation.4 | async-start | bytes 2097152 | tf_op jit(solution)/shard_map/all_to_all | solution.py:150
  199.6 0.7 fusion.56
  200.3 1.3 fusion.28
  201.6 1.3 fusion.30
  203.0 1.0 fusion.34
  204.0 1.0 fusion.35
  205.0 0.3 fusion.20
  205.3 21.3 %all-to-all-done.4 = bf16[64,8,1024]{2,1,0:T(8,128)(2,1)S(1)} async-done(((bf16[64,8,1024]{2,1,0:T(8,128)(2,1)}), bf16[64,8,1024]{2,1,0:T(8,128)(2,1)S(1)}, u32[]{:S(2)}, u32[]{:S(2)}) %all-to-all-start.4) | async-done | bytes 1048608 | tf_op jit(solution)/shard_map/all_to_all | solution.py:150
  226.6 0.6 gather_fusion
  227.1 0.9 fusion.36
  228.0 3.5 %reduce-scatter.2.cloned.1.call-done = f32[64,640]{1,0:T(8,128)} async-done(((f32[64,5120]{1,0:T(8,128)}), f32[64,640]{1,0:T(8,128)}) %reduce-scatter.2.cloned.1.call-update) | async-done | bytes 163856 | tf_op jit(solution)/shard_map/reduce_scatter | solution.py:161
  231.6 1.6 convert_element_type.80
  (49 shorter events, 2.2 us)
Async XLA Ops:
  7.2 20.7 %copy-start = (bf16[128,1024]{1,0:T(8,128)(2,1)S(1)}, bf16[128,1024]{1,0:T(8,128)(2,1)}, u32[]{:S(2)}) copy-start(bf16[128,1024]{1,0:T(8,128)(2,1)} %param.22) | copy-start | bytes 786436
  8.0 0.6 copy-start.7
  11.0 16.2 %copy-start.2 = (bf16[128,1024]{1,0:T(8,128)(2,1)S(1)}, bf16[128,1024]{1,0:T(8,128)(2,1)}, u32[]{:S(2)}) copy-start(bf16[128,1024]{1,0:T(8,128)(2,1)} %param.25) | copy-start | bytes 786436
  13.3 25.4 %all-to-all-start.1 = ((f32[64,8,1,8]{3,1,2,0:T(8,128)}), f32[64,8,1,8]{3,1,2,0:T(8,128)S(1)}, u32[]{:S(2)}, u32[]{:S(2)}) async-start(f32[64,8,1,8]{3,1,2,0:T(8,128)} %get-tuple-element.163), calls=%async_computation.1 | async-start | bytes 524288 | tf_op jit(solution)/shard_map/all_to_all | solution.py:143
  38.7 0.7 copy-start.4
  39.4 18.1 %all-to-all-start.3 = ((f32[64,8,1,8]{3,1,2,0:T(8,128)}), f32[64,8,1,8]{3,1,2,0:T(8,128)}, u32[]{:S(2)}, u32[]{:S(2)}) async-start(f32[64,8,1,8]{3,1,2,0:T(8,128)} %get-tuple-element.162), calls=%async_computation.3 | async-start | bytes 524288 | tf_op jit(solution)/shard_map/all_to_all | solution.py:144
  90.9 8.0 %copy-start.10 = (bf16[80,128]{1,0:T(8,128)(2,1)S(1)}, bf16[80,128]{1,0:T(8,128)(2,1)}, u32[]{:S(2)}) copy-start(bf16[80,128]{1,0:T(8,128)(2,1)} %param.21) | copy-start | bytes 61444
  90.9 8.0 %copy-start.11 = (bf16[80,128]{1,0:T(8,128)(2,1)S(1)}, bf16[80,128]{1,0:T(8,128)(2,1)}, u32[]{:S(2)}) copy-start(bf16[80,128]{1,0:T(8,128)(2,1)} %param.20) | copy-start | bytes 61444
  90.9 35.0 %copy-start.5 = (bf16[64,128]{1,0:T(8,128)(2,1)S(1)}, bf16[64,128]{1,0:T(8,128)(2,1)}, u32[]{:S(2)}) copy-start(bf16[64,128]{1,0:T(8,128)(2,1)} %param.19) | copy-start | bytes 49156
  90.9 35.0 %copy-start.6 = (bf16[64,128]{1,0:T(8,128)(2,1)S(1)}, bf16[64,128]{1,0:T(8,128)(2,1)}, u32[]{:S(2)}) copy-start(bf16[64,128]{1,0:T(8,128)(2,1)} %param.18) | copy-start | bytes 49156
  91.0 35.0 %all-to-all-start.2 = ((bf16[64,8,1024]{2,1,0:T(8,128)(2,1)}), bf16[64,8,1024]{2,1,0:T(8,128)(2,1)}, u32[]{:S(2)}, u32[]{:S(2)}) async-start(bf16[64,8,1024]{2,1,0:T(8,128)(2,1)} %get-tuple-element.164), calls=%async_computation.2 | async-start | bytes 2097152 | tf_op jit(solution)/shard_map/all_to_all | solution.py:140
  98.9 89.0 %all-gather.2.cloned.1.call-start = ((), (), s32[]{:S(2)}) async-start(), calls=%async_computation.6 | async-start | bytes 2662400 | tf_op jit(solution)/shard_map/all_gather | solution.py:159
  99.7 131.9 %reduce-scatter.2.cloned.1.call-start = ((), (), s32[]{:S(2)}) async-start(), calls=%async_computation.7 | async-start | bytes 1474560 | tf_op jit(solution)/shard_map/reduce_scatter | solution.py:161
  187.9 2.1 copy-start.1
  191.8 8.6 %copy-start.9 = (bf16[128,128]{1,0:T(8,128)(2,1)S(1)}, bf16[128,128]{1,0:T(8,128)(2,1)}, u32[]{:S(2)}) copy-start(bf16[128,128]{1,0:T(8,128)(2,1)} %param.23) | copy-start | bytes 98308
  191.8 9.8 %copy-start.3 = (bf16[128,1024]{1,0:T(8,128)(2,1)S(1)}, bf16[128,1024]{1,0:T(8,128)(2,1)}, u32[]{:S(2)}) copy-start(bf16[128,1024]{1,0:T(8,128)(2,1)} %param.25) | copy-start | bytes 786436
  191.8 9.8 %copy-start.8 = (bf16[128,128]{1,0:T(8,128)(2,1)S(1)}, bf16[128,128]{1,0:T(8,128)(2,1)}, u32[]{:S(2)}) copy-start(bf16[128,128]{1,0:T(8,128)(2,1)} %param.24) | copy-start | bytes 98308
  191.8 34.8 %all-to-all-start.4 = ((bf16[64,8,1024]{2,1,0:T(8,128)(2,1)}), bf16[64,8,1024]{2,1,0:T(8,128)(2,1)S(1)}, u32[]{:S(2)}, u32[]{:S(2)}) async-start(bf16[64,8,1024]{2,1,0:T(8,128)(2,1)} %bitcast.41), calls=%async_computation.4 | async-start | bytes 2097152 | tf_op jit(solution)/shard_map/all_to_all | solution.py:150
Sparse Core Ops, SparseCore 0:
  103.6 84.2 all-gather.1
  191.9 39.6 reduce-scatter.1
where the time goes:
time: 241 us; the launch traced here: 240 us
  waiting for transfers between devices  118 us (49%)
  starting transfers between devices  36.2 us (15%)
  blocking collectives  33.4 us (14%)
  local copies, waits for them, and re-layouts  17.7 us (7%)
  between operations  14.3 us (6%)
  matrix products  13.3 us (6%)
  other arithmetic  7.21 us (3%)
    all_gather x1, waiting for transfers between devices, body(): piece = lax.all_gather(stacked, 'dp', axis=1, tiled=True)  46.2 us
    all_to_all x1, blocking collectives, body(): lax.all_to_all(send_query, 'dp', split_axis=0, concat_axis=0, tiled=True)  33.4 us
    all_to_all x1, waiting for transfers between devices, body(): lax.all_to_all(send_grad, 'dp', split_axis=0, concat_axis=0, tiled=True)  26.2 us
    all_to_all x1, waiting for transfers between devices, body(): lax.all_to_all(prefix_dq, 'dp', split_axis=0, concat_axis=0, tiled=True)  21.3 us
    all_to_all x1, starting transfers between devices, body(): lax.all_to_all(send_norm, 'dp', split_axis=0, concat_axis=0, tiled=True)  13.9 us
    all_to_all x1, waiting for transfers between devices, body(): lax.all_to_all(send_norm, 'dp', split_axis=0, concat_axis=0, tiled=True)  10.2 us
    all_to_all x1, waiting for transfers between devices, body(): lax.all_to_all(send_delta, 'dp', split_axis=0, concat_axis=0, tiled=True)  10.1 us
    all_to_all x1, starting transfers between devices, body(): lax.all_to_all(send_grad, 'dp', split_axis=0, concat_axis=0, tiled=True)  7.95 us
  transfers between devices with their start and end apart: 6, of which 6 were waited for; matrix products, arithmetic and copies ran while one was open for 11% of the time, Pallas kernels for 0%

commit v1 on v0

v1 whole, which is shorter than its diff:
```python
import math

import jax
import jax.numpy as jnp
from jax import lax
from jax.experimental import pallas as pl
from jax.experimental.pallas import tpu as pltpu
from jax.sharding import PartitionSpec as P

HD = 128
HEADS = 8
LP = 64
LR = 8
SLOTS = 16
PAIRS = SLOTS // 2
NX, NZ, NC, NY = 4, 8, 2, 8
WROWS = 80
SCALE = 1.0 / math.sqrt(HD)
MESH = pl.DeviceIdType.MESH
BF, F32 = jnp.bfloat16, jnp.float32
Z_ORDER = (4, 3, 5, 2, 6, 1, 7)
Z_NEAR = (1, 7, 2, 6, 3, 5, 4)
X_ORDER = (2, 1, 3)
Y_ORDER = (4, 3, 5, 2, 6, 1, 7)
Y_NEAR = (1, 7, 2, 6, 3, 5, 4)


def dot_nt(a, b):
    return lax.dot_general(a, b, (((1,), (1,)), ((), ())), preferred_element_type=F32)


def dot_nn(a, b):
    return lax.dot_general(a, b, (((1,), (0,)), ((), ())), preferred_element_type=F32)


def dot_tn(a, b):
    return lax.dot_general(a, b, (((0,), (0,)), ((), ())), preferred_element_type=F32)


def spread_rows(rows):
    lane = lax.broadcasted_iota(jnp.int32, (HEADS, HD), 1) // 16
    head = lax.broadcasted_iota(jnp.int32, (HEADS, HD), 0)
    turned = [rows if k == 0 else pltpu.roll(rows, 16 * k, 1) for k in range(8)]
    out = []
    for pair in range(PAIRS):
        picked = jnp.zeros((HEADS, HD), F32)
        for h in range(HEADS):
            picked = jnp.where((head == h) & (lane == h), turned[(h - pair) % 8], picked)
        out.append(jnp.sum(picked, axis=0, keepdims=True))
    return jnp.concatenate(out, axis=0)


def kernel(
    pk_ref, pv_ref, kw_ref, vw_ref, q_ref, rk_ref, rv_ref, g_ref, lse_ref, delta_ref, prompt_ref, len_ref,
    dq_ref, drk_ref, drv_ref, out_ref,
    kv, wst, wbuf, q, g, rk, rv, lse, delta, lse_t, delta_t,
    own, sib, table, table_s, snd1, rcv1, snd2, rcv2, rcv3,
    load_sem, table_sem,
    kz_s, kz_r, kx_s, kx_r, kc_s, kc_r,
    w0_s, w0_r, wx_s, wx_r, wz_s, wz_r, wc_s, wc_r,
    rc_s, rc_r, rx_s, rx_r, rz_s, rz_r, ry_s, ry_r,
):
    me = lax.axis_index("dp")
    t = lax.axis_index("tensor")
    x, z, c = me // 16, (me // 2) % 8, me % 2

    def at(xx, zz, cc):
        return xx * 16 + zz * 2 + cc

    def xp(k):
        return (at((x + k) % NX, z, c), t)

    def zp(k):
        return (at(x, (z + k) % NZ, c), t)

    def yp(k):
        return (me, (t + k) % NY)

    other = (at(x, z, 1 - c), t)

    def remote(src, dst, s, r, dev):
        return pltpu.make_async_remote_copy(src_ref=src, dst_ref=dst, send_sem=s, recv_sem=r, device_id=dev, device_id_type=MESH)

    loads = [
        (pk_ref, kv.at[me, 0:LP]),
        (pv_ref, kv.at[me, LP : 2 * LP]),
        (kw_ref, wst.at[0:WROWS]),
        (vw_ref, wst.at[WROWS : 2 * WROWS]),
        (q_ref, q),
        (g_ref, g),
        (rk_ref, rk),
        (rv_ref, rv),
        (lse_ref, lse),
        (delta_ref, delta),
    ]
    loads = [pltpu.make_async_copy(a, b, load_sem.at[i]) for i, (a, b) in enumerate(loads)]
    for copy in loads:
        copy.start()

    w_to = (at((me % 4 + 1) % NX, t, (me // 4) % 2), me // 8)
    w_from = (8 * t + 4 * c + (x + 3) % 4, z)

    barrier = pltpu.get_barrier_semaphore()
    peers = [zp(k) for k in range(1, NZ)] + [xp(k) for k in range(1, NX)] + [yp(k) for k in range(1, NY)]
    peers += [other, w_to, w_from]
    for dev in peers:
        pl.semaphore_signal(barrier, inc=1, device_id=dev, device_id_type=MESH)
    loads[0].wait()
    loads[1].wait()
    loads[2].wait()
    loads[3].wait()
    pl.semaphore_wait(barrier, len(peers))

    sent = []

    def go(copy):
        copy.start()
        sent.append(copy)

    def kz(k):
        return remote(kv.at[me], kv.at[me], kz_s.at[k], kz_r.at[k], zp(k))

    def from_z(k):
        return at(x, (z - k + NZ) % NZ, c)

    def kx(kz_, k):
        p = from_z(kz_)
        return remote(kv.at[p], kv.at[p], kx_s.at[kz_, k], kx_r.at[kz_, k], xp(k))

    def kc(kz_, k):
        p = at((x - k + NX) % NX, (z - kz_ + NZ) % NZ, c)
        return remote(kv.at[p], kv.at[p], kc_s.at[kz_, k], kc_r.at[kz_, k], other)

    def kc_in(kz_, k):
        p = at((x - k + NX) % NX, (z - kz_ + NZ) % NZ, 1 - c)
        return remote(kv.at[p], kv.at[p], kc_s.at[kz_, k], kc_r.at[kz_, k], other)

    def kz_in(k):
        p = from_z(k)
        return remote(kv.at[p], kv.at[p], kz_s.at[k], kz_r.at[k], zp(k))

    def kx_in(kz_, k):
        p = at((x - k + NX) % NX, (z - kz_ + NZ) % NZ, c)
        return remote(kv.at[p], kv.at[p], kx_s.at[kz_, k], kx_r.at[kz_, k], xp(k))

    for k in Z_ORDER:
        go(kz(k))
    for k in X_ORDER:
        go(kx(0, k))
    go(kc(0, 0))

    wt_x, wt_z, wt_c = (me % 4 + 1) % NX, t, (me // 4) % 2
    go(remote(wst, wbuf.at[wt_c, wt_z, wt_x], w0_s, w0_r, w_to))

    lane = lax.broadcasted_iota(jnp.int32, (1, HD), 1)
    rows = []
    for base in (me, at(x, z, 1 - c)):
        found = jnp.full((1, HD), SLOTS, jnp.int32)
        for s in range(SLOTS):
            found = jnp.where(lane == prompt_ref[base * SLOTS + s], s, found)
        rows.append(found)
    table[0:1, :] = rows[0]
    table[1:2, :] = rows[1]
    table_copy = pltpu.make_async_copy(table, table_s, table_sem)
    table_copy.start()
    own[SLOTS] = jnp.zeros((2 * LP, HD), BF)
    sib[SLOTS] = jnp.zeros((2 * LP, HD), BF)

    for copy in loads[4:]:
        copy.wait()
    lse_t[...] = spread_rows(lse[...])
    delta_t[...] = spread_rows(delta[...])

    for k in Z_NEAR:
        kz_in(k).wait_recv()
        for k2 in X_ORDER:
            go(kx(k, k2))
        go(kc(k, 0))

    w_mine = remote(wst, wbuf.at[c, z, x], w0_s, w0_r, w_to)
    w_mine.wait_recv()

    def wx(k):
        return remote(wbuf.at[c, z, x], wbuf.at[c, z, x], wx_s.at[k], wx_r.at[k], xp(k))

    def wx_in(k):
        xx = (x - k + NX) % NX
        return remote(wbuf.at[c, z, xx], wbuf.at[c, z, xx], wx_s.at[k], wx_r.at[k], xp(k))

    for k in X_ORDER:
        go(wx(k))

    for k in (0,) + Z_NEAR:
        for k2 in (1, 3, 2):
            kx_in(k, k2).wait_recv()
            go(kc(k, k2))

    def wz(k, way):
        zz = (z - (k - 1) * way + NZ) % NZ
        return remote(wbuf.at[c, zz], wbuf.at[c, zz], wz_s.at[(k * way) % NZ], wz_r.at[(k * way) % NZ], zp(way % NZ))

    def wz_in(k, way):
        zz = (z - k * way + NZ) % NZ
        return remote(wbuf.at[c, zz], wbuf.at[c, zz], wz_s.at[(k * way) % NZ], wz_r.at[(k * way) % NZ], zp(way % NZ))

    def wc(k):
        zz = (z - k + NZ) % NZ
        return remote(wbuf.at[c, zz], wbuf.at[c, zz], wc_s.at[k], wc_r.at[k], other)

    def wc_in(k):
        zz = (z - k + NZ) % NZ
        return remote(wbuf.at[1 - c, zz], wbuf.at[1 - c, zz], wc_s.at[k], wc_r.at[k], other)

    def w_hop(k):
        for way in (1, -1):
            if k > 1 and (way == 1 or k <= 4):
                wz_in(k - 1, way).wait_recv()
        for way in (1, -1):
            if k <= (4 if way == 1 else 3):
                go(wz(k, way))
        if k == 1:
            go(wc(0))
        else:
            for way in (1, -1):
                if way == 1 or k <= 4:
                    go(wc(((k - 1) * way) % NZ))

    for k in X_ORDER:
        wx_in(k).wait_recv()
    w_hop(1)

    for k in range(NZ):
        for k2 in range(NX):
            kc_in(k, k2).wait_recv()

    key_row = lax.broadcasted_iota(jnp.int32, (2 * LP + 16, HD), 0)
    column = lax.broadcasted_iota(jnp.int32, (2 * LP + 16, HD), 1)
    col_r, col_t = (column // LR) % 2, column % LR
    in_own = key_row >= 2 * LP
    row_r = jnp.where(in_own, (key_row - 2 * LP) // LR, key_row // LP)
    seen = (row_r == col_r) & (jnp.logical_not(in_own) | ((key_row % LR) <= col_t))
    col_r1, col_t1 = col_r[0:1], col_t[0:1]

    def one_pair(pair):
        base = pl.multiple_of(pair * 16, 16)
        p0, p1 = prompt_ref[me * SLOTS + 2 * pair], prompt_ref[me * SLOTS + 2 * pair + 1]
        l0, l1 = len_ref[2 * pair], len_ref[2 * pair + 1]
        kv0, kv1 = kv[p0], kv[p1]
        keys = jnp.concatenate([kv0[:LP], kv1[:LP], rk[pl.ds(base, 16)]], axis=0)
        values = jnp.concatenate([kv0[LP:], kv1[LP:], rv[pl.ds(base, 16)]], axis=0)
        qp = jnp.concatenate([q[pl.ds(base, 16), h * HD : (h + 1) * HD] for h in range(HEADS)], axis=0)
        gp = jnp.concatenate([g[pl.ds(base, 16), h * HD : (h + 1) * HD] for h in range(HEADS)], axis=0)
        live = col_t1 < jnp.where(col_r1 == 0, l0, l1)
        scores = dot_nt(keys, qp) * SCALE
        probs = jnp.exp(scores - lse_t[pl.ds(pair, 1)])
        probs = jnp.where(seen & live, probs, 0.0)
        dprob = dot_nt(values, gp)
        dscore = (probs * (dprob - delta_t[pl.ds(pair, 1)])).astype(BF)
        dv = dot_nn(probs.astype(BF), gp)
        dk = dot_nn(dscore, qp)
        dq = dot_tn(dscore, keys) * SCALE
        for r in range(2):
            own[2 * pair + r, 0:LP] = dk[r * LP : (r + 1) * LP].astype(BF)
            own[2 * pair + r, LP : 2 * LP] = dv[r * LP : (r + 1) * LP].astype(BF)
        drk_ref[pl.ds(base, 16)] = (dk[2 * LP :] * SCALE).astype(BF)
        drv_ref[pl.ds(base, 16)] = dv[2 * LP :].astype(BF)
        for h in range(HEADS):
            dq_ref[pl.ds(base, 16), h * HD : (h + 1) * HD] = dq[h * 16 : (h + 1) * 16].astype(BF)

    def rc(i):
        return remote(own.at[pl.ds(4 * i, 4)], sib.at[pl.ds(4 * i, 4)], rc_s.at[i], rc_r.at[i], other)

    for i in range(4):
        one_pair(2 * i)
        one_pair(2 * i + 1)
        go(rc(i))
        if i == 1:
            w_hop(2)
        if i == 3:
            w_hop(3)

    table_copy.wait()
    for i in range(4):
        rc(i).wait_recv()

    def both_cores(j):
        return own[table_s[0, j]].astype(F32) + sib[table_s[1, j]].astype(F32)

    def rx(k, half):
        part = pl.ds(4 * half, 4)
        return remote(snd1.at[k - 1, part], rcv1.at[k - 1, part], rx_s.at[k - 1, half], rx_r.at[k - 1, half], xp(k))

    ranks = Z_ORDER + (0,)
    for half in range(2):
        for k in X_ORDER:
            for i in range(4 * half, 4 * half + 4):
                j = at((x + k) % NX, (z + ranks[i]) % NZ, c)
                snd1[k - 1, i] = both_cores(j).astype(BF)
            go(rx(k, half))

    def rz(i):
        k = ranks[i]
        return remote(snd2.at[i], rcv2.at[i], rz_s.at[i], rz_r.at[i], zp(k))

    w_hop(4)
    mine = None
    for half in range(2):
        for k in X_ORDER:
            rx(k, half).wait_recv()
        for i in range(4 * half, 4 * half + 4):
            total = both_cores(at(x, (z + ranks[i]) % NZ, c))
            for k in range(NX - 1):
                total = total + rcv1[k, i].astype(F32)
            if i < NZ - 1:
                snd2[i] = total.astype(BF)
                go(rz(i))
            else:
                mine = total
    wz_in(4, 1).wait_recv()
    go(wc(4))
    for i in range(NZ - 1):
        rz(i).wait_recv()
        mine = mine + rcv2[i].astype(F32)
    row = lax.broadcasted_iota(jnp.int32, (2 * LP, HD), 0)
    rcv3[0] = jnp.where(row < LP, mine * SCALE, mine).astype(BF)

    def ry(k):
        return remote(rcv3.at[0], rcv3.at[k], ry_s.at[k], ry_r.at[k], yp(k))

    for k in Y_ORDER:
        go(ry(k))
    for k in range(NZ):
        wc_in(k).wait_recv()

    def project(k):
        head = (t - k + NY) % NY
        part = rcv3[k]
        both = jnp.concatenate([part[:LP], part[LP:]], axis=1)
        weights = []
        for cc in range(NC):
            for j in range(4):
                block = wbuf[cc, head, (j + 1) % 4]
                weights.append(jnp.concatenate([block[:WROWS], block[WROWS:]], axis=1))
        return dot_nt(both, jnp.concatenate(weights, axis=0))

    acc = project(0)
    for k in Y_NEAR:
        ry(k).wait_recv()
        acc = acc + project(k)
    out_ref[...] = acc.astype(BF)

    for copy in sent:
        copy.wait_send()


def body(*args):
    vmem = pl.BlockSpec(memory_space=pltpu.VMEM)
    smem = pl.BlockSpec(memory_space=pltpu.SMEM)
    hbm = pl.BlockSpec(memory_space=pl.ANY)
    rows = SLOTS * LR
    dma = pltpu.SemaphoreType.DMA
    return pl.pallas_call(
        kernel,
        out_shape=(
            jax.ShapeDtypeStruct((rows, HEADS * HD), BF),
            jax.ShapeDtypeStruct((rows, HD), BF),
            jax.ShapeDtypeStruct((rows, HD), BF),
            jax.ShapeDtypeStruct((LP, 8 * WROWS), BF),
        ),
        in_specs=[hbm] * 10 + [smem] * 2,
        out_specs=(vmem,) * 4,
        scratch_shapes=[
            pltpu.VMEM((64, 2 * LP, HD), BF),
            pltpu.VMEM((2 * WROWS, HD), BF),
            pltpu.VMEM((NC, NZ, NX, 2 * WROWS, HD), BF),
            pltpu.VMEM((rows, HEADS * HD), BF),
            pltpu.VMEM((rows, HEADS * HD), BF),
            pltpu.VMEM((rows, HD), BF),
            pltpu.VMEM((rows, HD), BF),
            pltpu.VMEM((HEADS, rows), F32),
            pltpu.VMEM((HEADS, rows), F32),
            pltpu.VMEM((PAIRS, HD), F32),
            pltpu.VMEM((PAIRS, HD), F32),
            pltpu.VMEM((SLOTS + 1, 2 * LP, HD), BF),
            pltpu.VMEM((SLOTS + 1, 2 * LP, HD), BF),
            pltpu.VMEM((8, HD), jnp.int32),
            pltpu.SMEM((8, HD), jnp.int32),
            pltpu.VMEM((NX - 1, NZ, 2 * LP, HD), BF),
            pltpu.VMEM((NX - 1, NZ, 2 * LP, HD), BF),
            pltpu.VMEM((NZ - 1, 2 * LP, HD), BF),
            pltpu.VMEM((NZ - 1, 2 * LP, HD), BF),
            pltpu.VMEM((NY, 2 * LP, HD), BF),
            dma((10,)),
            dma,
            dma((NZ,)), dma((NZ,)), dma((NZ, NX)), dma((NZ, NX)), dma((NZ, NX)), dma((NZ, NX)),
            dma, dma, dma((NX,)), dma((NX,)), dma((NZ,)), dma((NZ,)), dma((NZ,)), dma((NZ,)),
            dma((4,)), dma((4,)), dma((NX - 1, 2)), dma((NX - 1, 2)), dma((NZ,)), dma((NZ,)), dma((NY,)), dma((NY,)),
        ],
        compiler_params=pltpu.CompilerParams(
            collective_id=0, has_side_effects=True, vmem_limit_bytes=32 << 20
        ),
        name="attention_back",
    )(*args)


def solution(mesh):
    split = P("dp", "tensor")
    return jax.shard_map(
        body,
        mesh=mesh,
        in_specs=(split,) * 8 + (P("tensor", "dp"),) * 2 + (P(), P("dp")),
        out_specs=(split,) * 4,
        check_vma=False,
    )
```

time: 241 us -> 91 us (0.38)
  the two profiles are of different devices: /device:TPU:2 before, /device:TPU:8 now
where the time goes in v1:
time: 91 us; the launch traced here: 90.3 us
  Pallas kernels  78.1 us (86%)
  local copies, waits for them, and re-layouts  11.6 us (13%)
    pallas_call x1, Pallas kernels, body(): pl.pallas_call(kernel, out_shape=(jax.ShapeDtypeStruct((rows, HEADS * HD)...  78.1 us
    unnamed x28, local copies, waits for them, and re-layouts  11.6 us

profile of v1, /device:TPU:8, one launch (start us, length us, event | category | flops | bytes accessed | tf_op | source)
XLA Modules:
  0.0 90.3 jit_solution(6895002043318012570)
XLA Ops:
  0.6 0.0 copy-start
  0.6 0.9 %copy-done = bf16[128,1024]{1,0:T(8,128)(2,1)S(1)} copy-done((bf16[128,1024]{1,0:T(8,128)(2,1)S(1)}, bf16[128,1024]{1,0:T(8,128)(2,1)}, u32[]{:S(2)}) %copy-start) | copy-done | bytes 262168
  1.6 0.0 copy-start.1
  1.6 0.9 %copy-done.1 = bf16[128,1024]{1,0:T(8,128)(2,1)S(1)} copy-done((bf16[128,1024]{1,0:T(8,128)(2,1)S(1)}, bf16[128,1024]{1,0:T(8,128)(2,1)}, u32[]{:S(2)}) %copy-start.1) | copy-done | bytes 262168
  2.5 0.0 copy-start.2
  2.5 0.8 copy-done.2
  3.3 0.0 copy-start.3
  3.3 0.8 copy-done.3
  4.1 0.0 copy-start.4
  4.1 0.7 copy-done.4
  4.8 0.0 copy-start.5
  4.8 0.7 copy-done.5
  5.5 0.0 copy-start.6
  5.5 0.7 copy-done.6
  6.2 0.0 copy-start.7
  6.2 0.7 copy-done.7
  6.9 0.0 copy-start.8
  6.9 0.7 copy-done.8
  7.6 0.0 copy-start.9
  7.6 0.7 copy-done.9
  8.3 0.0 copy-start.10
  8.3 0.7 copy-done.10
  9.0 0.0 copy-start.11
  9.0 0.7 copy-done.11
  9.7 78.1 %attention_back.1 = (bf16[128,1024]{1,0:T(8,128)(2,1)S(1)}, bf16[128,128]{1,0:T(8,128)(2,1)S(1)}, bf16[128,128]{1,0:T(8,128)(2,1)S(1)}, bf16[64,640]{1,0:T(8,128)(2,1)S(1)}) custom-call(bf16[64,128]{1,0:T(8,128)(2,1)S(1)} %copy-done.6, bf16[64,128]{1,0:T(8,128)(2,1)S(1)} %copy-done.7, bf16[80,128]{1,0:T(8,128)(2,1)S(1)} %copy-done.4, ...), custom_call_target="tpu_custom_call" | custom-call | tf_op jit(solution)/shard_map/attention_back/pallas_call | solution.py:362
  87.8 0.7 copy.20
  88.5 0.6 copy.21
  89.1 0.6 copy.22
  89.7 0.6 copy.23
Async XLA Ops:
  0.6 1.0 %copy-start = (bf16[128,1024]{1,0:T(8,128)(2,1)S(1)}, bf16[128,1024]{1,0:T(8,128)(2,1)}, u32[]{:S(2)}) copy-start(bf16[128,1024]{1,0:T(8,128)(2,1)} %q_ref.1) | copy-start | bytes 786436
  1.6 0.9 %copy-start.1 = (bf16[128,1024]{1,0:T(8,128)(2,1)S(1)}, bf16[128,1024]{1,0:T(8,128)(2,1)}, u32[]{:S(2)}) copy-start(bf16[128,1024]{1,0:T(8,128)(2,1)} %g_ref.1) | copy-start | bytes 786436
  2.5 0.8 copy-start.2
  3.3 0.8 copy-start.3
  4.1 0.7 copy-start.4
  4.8 0.7 copy-start.5
  5.5 0.7 copy-start.6
  6.2 0.7 copy-start.7
  6.9 0.7 copy-start.8
  7.6 0.7 copy-start.9
  8.3 0.7 copy-start.10
  9.0 0.7 copy-start.11

commit v2 on v1

v2 whole, which is shorter than its diff:
```python
import math

import jax
import jax.numpy as jnp
from jax import lax
from jax.experimental import pallas as pl
from jax.experimental.pallas import tpu as pltpu
from jax.sharding import PartitionSpec as P

HD = 128
HEADS = 8
LP = 64
LR = 8
SLOTS = 16
PAIRS = SLOTS // 2
NX, NZ, NC, NY = 4, 8, 2, 8
WROWS = 80
SCALE = 1.0 / math.sqrt(HD)
MESH = pl.DeviceIdType.MESH
BF, F32 = jnp.bfloat16, jnp.float32
Z_RANKS = (0, 1, 7, 2, 6, 3, 5, 4)
Z_FAR = Z_RANKS[:0:-1]
X_ORDER = (2, 1, 3)
Y_ORDER = (4, 3, 5, 2, 6, 1, 7)
Y_NEAR = (1, 7, 2, 6, 3, 5, 4)


def dot_nt(a, b):
    return lax.dot_general(a, b, (((1,), (1,)), ((), ())), preferred_element_type=F32)


def dot_nn(a, b):
    return lax.dot_general(a, b, (((1,), (0,)), ((), ())), preferred_element_type=F32)


def dot_tn(a, b):
    return lax.dot_general(a, b, (((0,), (0,)), ((), ())), preferred_element_type=F32)


def rank(k):
    return jnp.where(k == 0, 0, jnp.where(k <= 4, 2 * k - 1, 16 - 2 * k))


def spread_rows(rows):
    lane = lax.broadcasted_iota(jnp.int32, (HEADS, HD), 1) // 16
    head = lax.broadcasted_iota(jnp.int32, (HEADS, HD), 0)
    turned = [rows if k == 0 else pltpu.roll(rows, 16 * k, 1) for k in range(8)]
    out = []
    for pair in range(PAIRS):
        picked = jnp.zeros((HEADS, HD), F32)
        for h in range(HEADS):
            picked = jnp.where((head == h) & (lane == h), turned[(h - pair) % 8], picked)
        out.append(jnp.sum(picked, axis=0, keepdims=True))
    return jnp.concatenate(out, axis=0)


def kernel(
    pk_ref, pv_ref, kw_ref, vw_ref, q_ref, rk_ref, rv_ref, g_ref, lse_ref, delta_ref, prompt_in, len_in,
    dq_ref, drk_ref, drv_ref, out_ref,
    prompt_ref, len_ref, kv, wst, wbuf, q, g, rk, rv, lse, delta, lse_t, delta_t,
    own, sib, table, table_s, snd1, rcv1, snd2, rcv2, rcv3,
    load_sem, table_sem,
    kz_s, kz_r, kx_s, kx_r, kc_s, kc_r,
    w0_s, w0_r, wx_s, wx_r, wz_s, wz_r, wc_s, wc_r,
    rc_s, rc_r, rx_s, rx_r, rz_s, rz_r, ry_s, ry_r,
):
    me = lax.axis_index("dp")
    t = lax.axis_index("tensor")
    x, z, c = me // 16, (me // 2) % 8, me % 2

    def at(xx, zz, cc):
        return xx * 16 + zz * 2 + cc

    def xp(k):
        return (at((x + k) % NX, z, c), t)

    def zp(k):
        return (at(x, (z + k) % NZ, c), t)

    def yp(k):
        return (me, (t + k) % NY)

    other = (at(x, z, 1 - c), t)

    def remote(src, dst, s, r, dev):
        return pltpu.make_async_remote_copy(src_ref=src, dst_ref=dst, send_sem=s, recv_sem=r, device_id=dev, device_id_type=MESH)

    loads = [
        (pk_ref, kv.at[c, x, 0, 0:LP]),
        (pv_ref, kv.at[c, x, 0, LP : 2 * LP]),
        (kw_ref, wst.at[0:WROWS]),
        (vw_ref, wst.at[WROWS : 2 * WROWS]),
        (q_ref, q),
        (g_ref, g),
        (rk_ref, rk),
        (rv_ref, rv),
        (lse_ref, lse),
        (delta_ref, delta),
        (prompt_in, prompt_ref),
        (len_in, len_ref),
    ]
    loads = [pltpu.make_async_copy(a, b, load_sem.at[i]) for i, (a, b) in enumerate(loads)]
    for copy in loads:
        copy.start()

    w_to = (at((me % 4 + 1) % NX, t, (me // 4) % 2), me // 8)
    w_from = (8 * t + 4 * c + (x + 3) % 4, z)

    barrier = pltpu.get_barrier_semaphore()
    peers = [zp(k) for k in range(1, NZ)] + [xp(k) for k in range(1, NX)] + [yp(k) for k in range(1, NY)]
    peers += [other, w_to, w_from]
    for dev in peers:
        pl.semaphore_signal(barrier, inc=1, device_id=dev, device_id_type=MESH)
    loads[0].wait()
    loads[1].wait()
    loads[2].wait()
    loads[3].wait()
    pl.semaphore_wait(barrier, len(peers))

    sent = []

    def go(copy):
        copy.start()
        sent.append(copy)

    wt_c, wt_z, wt_x = (me // 4) % 2, t, (me % 4 + 1) % NX

    def wz(i):
        return remote(wbuf.at[c, x, 0], wbuf.at[c, x, i], wz_s.at[i], wz_r.at[i], zp(Z_RANKS[i]))

    def wx(k):
        return remote(wbuf.at[c, x], wbuf.at[c, x], wx_s.at[k], wx_r.at[k], xp(k))

    def wx_in(k):
        dst = wbuf.at[c, (x - k + NX) % NX]
        return remote(dst, dst, wx_s.at[k], wx_r.at[k], xp(k))

    def wc(k):
        group = wbuf.at[c, (x - k + NX) % NX]
        return remote(group, group, wc_s.at[k], wc_r.at[k], other)

    def wc_in(k):
        group = wbuf.at[1 - c, (x - k + NX) % NX]
        return remote(group, group, wc_s.at[k], wc_r.at[k], other)

    def weights(step):
        if step == 0:
            go(remote(wst, wbuf.at[wt_c, wt_x, 0], w0_s, w0_r, w_to))
        elif step == 1:
            remote(wst, wbuf.at[c, x, 0], w0_s, w0_r, w_to).wait_recv()
            for i in range(NZ - 1, 0, -1):
                go(wz(i))
        elif step == 2:
            for i in range(1, NZ):
                wz(i).wait_recv()
            for k in X_ORDER:
                go(wx(k))
            go(wc(0))
        elif step == 3:
            for k in (1, 3, 2):
                wx_in(k).wait_recv()
                go(wc(k))
        else:
            for k in range(NX):
                wc_in(k).wait_recv()

    def kz(i):
        return remote(kv.at[c, x, 0], kv.at[c, x, i], kz_s.at[i], kz_r.at[i], zp(Z_RANKS[i]))

    def half_of(cc, xx, half):
        return kv.at[cc, xx, pl.ds(4 * half, 4)]

    def kx(k, half):
        group = half_of(c, x, half)
        return remote(group, group, kx_s.at[k, half], kx_r.at[k, half], xp(k))

    def kx_in(k, half):
        group = half_of(c, (x - k + NX) % NX, half)
        return remote(group, group, kx_s.at[k, half], kx_r.at[k, half], xp(k))

    def kc(k, half):
        group = half_of(c, (x - k + NX) % NX, half)
        return remote(group, group, kc_s.at[k, half], kc_r.at[k, half], other)

    def kc_in(k, half):
        group = half_of(1 - c, (x - k + NX) % NX, half)
        return remote(group, group, kc_s.at[k, half], kc_r.at[k, half], other)

    for i in range(NZ - 1, 0, -1):
        go(kz(i))
    weights(0)

    for copy in loads[4:]:
        copy.wait()

    lane = lax.broadcasted_iota(jnp.int32, (1, HD), 1)
    rows = []
    for base in (me, at(x, z, 1 - c)):
        found = jnp.full((1, HD), SLOTS, jnp.int32)
        for s in range(SLOTS):
            found = jnp.where(lane == prompt_ref[base * SLOTS + s], s, found)
        rows.append(found)
    table[0:1, :] = rows[0]
    table[1:2, :] = rows[1]
    table_copy = pltpu.make_async_copy(table, table_s, table_sem)
    table_copy.start()
    own[SLOTS] = jnp.zeros((2 * LP, HD), BF)
    sib[SLOTS] = jnp.zeros((2 * LP, HD), BF)

    lse_t[...] = spread_rows(lse[...])
    delta_t[...] = spread_rows(delta[...])

    for half in range(2):
        for i in range(max(4 * half, 1), 4 * half + 4):
            kz(i).wait_recv()
        for k in X_ORDER:
            go(kx(k, half))
        go(kc(0, half))
    weights(1)
    for half in range(2):
        for k in (1, 3, 2):
            kx_in(k, half).wait_recv()
            go(kc(k, half))
    for half in range(2):
        for k in range(NX):
            kc_in(k, half).wait_recv()

    key_row = lax.broadcasted_iota(jnp.int32, (2 * LP + 16, HD), 0)
    column = lax.broadcasted_iota(jnp.int32, (2 * LP + 16, HD), 1)
    col_r, col_t = (column // LR) % 2, column % LR
    in_own = key_row >= 2 * LP
    row_r = jnp.where(in_own, (key_row - 2 * LP) // LR, key_row // LP)
    seen = (row_r == col_r) & (jnp.logical_not(in_own) | ((key_row % LR) <= col_t))
    col_r1, col_t1 = col_r[0:1], col_t[0:1]

    def one_pair(pair):
        base = pl.multiple_of(pair * 16, 16)
        p0, p1 = prompt_ref[me * SLOTS + 2 * pair], prompt_ref[me * SLOTS + 2 * pair + 1]
        l0, l1 = len_ref[2 * pair], len_ref[2 * pair + 1]
        kv0, kv1 = (kv[p % 2, p // 16, rank((z - (p // 2) % 8 + NZ) % NZ)] for p in (p0, p1))
        keys = jnp.concatenate([kv0[:LP], kv1[:LP], rk[pl.ds(base, 16)]], axis=0)
        values = jnp.concatenate([kv0[LP:], kv1[LP:], rv[pl.ds(base, 16)]], axis=0)
        qp = jnp.concatenate([q[pl.ds(base, 16), h * HD : (h + 1) * HD] for h in range(HEADS)], axis=0)
        gp = jnp.concatenate([g[pl.ds(base, 16), h * HD : (h + 1) * HD] for h in range(HEADS)], axis=0)
        live = col_t1 < jnp.where(col_r1 == 0, l0, l1)
        scores = dot_nt(keys, qp) * SCALE
        probs = jnp.exp(scores - lse_t[pl.ds(pair, 1)])
        probs = jnp.where(seen & live, probs, 0.0)
        dprob = dot_nt(values, gp)
        dscore = (probs * (dprob - delta_t[pl.ds(pair, 1)])).astype(BF)
        dv = dot_nn(probs.astype(BF), gp)
        dk = dot_nn(dscore, qp)
        dq = dot_tn(dscore, keys) * SCALE
        for r in range(2):
            own[2 * pair + r, 0:LP] = dk[r * LP : (r + 1) * LP].astype(BF)
            own[2 * pair + r, LP : 2 * LP] = dv[r * LP : (r + 1) * LP].astype(BF)
        drk_ref[pl.ds(base, 16)] = (dk[2 * LP :] * SCALE).astype(BF)
        drv_ref[pl.ds(base, 16)] = dv[2 * LP :].astype(BF)
        for h in range(HEADS):
            dq_ref[pl.ds(base, 16), h * HD : (h + 1) * HD] = dq[h * 16 : (h + 1) * 16].astype(BF)

    def rc(i):
        return remote(own.at[pl.ds(4 * i, 4)], sib.at[pl.ds(4 * i, 4)], rc_s.at[i], rc_r.at[i], other)

    for i in range(4):
        one_pair(2 * i)
        one_pair(2 * i + 1)
        go(rc(i))
        if i == 1:
            weights(2)

    table_copy.wait()
    for i in range(4):
        rc(i).wait_recv()

    def both_cores(j, part):
        rows = slice(LP * part, LP * (part + 1))
        return own[table_s[0, j], rows].astype(F32) + sib[table_s[1, j], rows].astype(F32)

    def rx(k, part):
        return remote(snd1.at[part, k - 1], rcv1.at[part, k - 1], rx_s.at[part, k - 1], rx_r.at[part, k - 1], xp(k))

    def rz(i, part):
        return remote(snd2.at[part, i], rcv2.at[part, i], rz_s.at[part, i], rz_r.at[part, i], zp(Z_RANKS[i]))

    def ry(k, part):
        rows = pl.ds(LP * part, LP)
        return remote(rcv3.at[0, rows], rcv3.at[k, rows], ry_s.at[part, k], ry_r.at[part, k], yp(k))

    def ahead(i):
        return (z + Z_RANKS[i]) % NZ

    for part in range(2):
        for k in X_ORDER:
            for i in range(NZ):
                snd1[part, k - 1, i] = both_cores(at((x + k) % NX, ahead(i), c), part).astype(BF)
            go(rx(k, part))

    mine = [None, None]
    for part in range(2):
        for k in (1, 3, 2):
            rx(k, part).wait_recv()
        for i in range(NZ - 1, -1, -1):
            total = both_cores(at(x, ahead(i), c), part)
            for k in range(NX - 1):
                total = total + rcv1[part, k, i].astype(F32)
            if i:
                snd2[part, i] = total.astype(BF)
                go(rz(i, part))
            else:
                mine[part] = total
    weights(3)
    for part in range(2):
        for i in range(1, NZ):
            rz(i, part).wait_recv()
            mine[part] = mine[part] + rcv2[part, i].astype(F32)
        rcv3[0, LP * part : LP * (part + 1)] = (mine[part] * SCALE if part == 0 else mine[part]).astype(BF)
        for k in Y_ORDER:
            go(ry(k, part))
    weights(4)

    def project(k):
        head = (t - k + NY) % NY
        place = rank((z - head + NZ) % NZ)
        grads = rcv3[k]
        both = jnp.concatenate([grads[:LP], grads[LP:]], axis=1)
        weights = []
        for cc in range(NC):
            for j in range(4):
                block = wbuf[cc, (j + 1) % NX, place]
                weights.append(jnp.concatenate([block[:WROWS], block[WROWS:]], axis=1))
        return dot_nt(both, jnp.concatenate(weights, axis=0))

    acc = project(0)
    for k in Y_NEAR:
        for part in range(2):
            ry(k, part).wait_recv()
        acc = acc + project(k)
    out_ref[...] = acc.astype(BF)

    for copy in sent:
        copy.wait_send()


def body(*args):
    vmem = pl.BlockSpec(memory_space=pltpu.VMEM)
    hbm = pl.BlockSpec(memory_space=pl.ANY)
    rows = SLOTS * LR
    dma = pltpu.SemaphoreType.DMA
    return pl.pallas_call(
        kernel,
        out_shape=(
            jax.ShapeDtypeStruct((rows, HEADS * HD), BF),
            jax.ShapeDtypeStruct((rows, HD), BF),
            jax.ShapeDtypeStruct((rows, HD), BF),
            jax.ShapeDtypeStruct((LP, 8 * WROWS), BF),
        ),
        in_specs=[hbm] * 12,
        out_specs=(vmem,) * 4,
        scratch_shapes=[
            pltpu.SMEM((64 * SLOTS,), jnp.int32),
            pltpu.SMEM((SLOTS,), jnp.int32),
            pltpu.VMEM((NC, NX, NZ, 2 * LP, HD), BF),
            pltpu.VMEM((2 * WROWS, HD), BF),
            pltpu.VMEM((NC, NX, NZ, 2 * WROWS, HD), BF),
            pltpu.VMEM((rows, HEADS * HD), BF),
            pltpu.VMEM((rows, HEADS * HD), BF),
            pltpu.VMEM((rows, HD), BF),
            pltpu.VMEM((rows, HD), BF),
            pltpu.VMEM((HEADS, rows), F32),
            pltpu.VMEM((HEADS, rows), F32),
            pltpu.VMEM((PAIRS, HD), F32),
            pltpu.VMEM((PAIRS, HD), F32),
            pltpu.VMEM((SLOTS + 1, 2 * LP, HD), BF),
            pltpu.VMEM((SLOTS + 1, 2 * LP, HD), BF),
            pltpu.VMEM((8, HD), jnp.int32),
            pltpu.SMEM((8, HD), jnp.int32),
            pltpu.VMEM((2, NX - 1, NZ, LP, HD), BF),
            pltpu.VMEM((2, NX - 1, NZ, LP, HD), BF),
            pltpu.VMEM((2, NZ, LP, HD), BF),
            pltpu.VMEM((2, NZ, LP, HD), BF),
            pltpu.VMEM((NY, 2 * LP, HD), BF),
            dma((12,)),
            dma,
            dma((NZ,)), dma((NZ,)), dma((NX, 2)), dma((NX, 2)), dma((NX, 2)), dma((NX, 2)),
            dma, dma, dma((NX,)), dma((NX,)), dma((NZ,)), dma((NZ,)), dma((NX,)), dma((NX,)),
            dma((4,)), dma((4,)), dma((2, NX - 1)), dma((2, NX - 1)), dma((2, NZ)), dma((2, NZ)), dma((2, NY)), dma((2, NY)),
        ],
        compiler_params=pltpu.CompilerParams(
            collective_id=0, has_side_effects=True, vmem_limit_bytes=62 << 20
        ),
        name="attention_back",
    )(*args)


def solution(mesh):
    split = P("dp", "tensor")
    return jax.shard_map(
        body,
        mesh=mesh,
        in_specs=(split,) * 8 + (P("tensor", "dp"),) * 2 + (P(), P("dp")),
        out_specs=(split,) * 4,
        check_vma=False,
    )
```

time: 91 us -> 89 us (0.978)
  the two profiles are of different devices: /device:TPU:8 before, /device:TPU:2 now
where the time goes in v2:
time: 89 us; the launch traced here: 88.8 us
  Pallas kernels  84.6 us (95%)
  local copies, waits for them, and re-layouts  3.56 us (4%)
    pallas_call x1, Pallas kernels, body(): pl.pallas_call(kernel, out_shape=(jax.ShapeDtypeStruct((rows, HEADS * HD)...  84.6 us
    unnamed x10, local copies, waits for them, and re-layouts  3.56 us

profile of v2, /device:TPU:2, one launch (start us, length us, event | category | flops | bytes accessed | tf_op | source)
XLA Modules:
  0.0 88.8 jit_solution(17653317615856652175)
XLA Ops:
  0.6 84.6 %attention_back.1 = (bf16[128,1024]{1,0:T(8,128)(2,1)}, bf16[128,128]{1,0:T(8,128)(2,1)}, bf16[128,128]{1,0:T(8,128)(2,1)}, bf16[64,640]{1,0:T(8,128)(2,1)}) custom-call(bf16[64,128]{1,0:T(8,128)(2,1)} %pk_ref.1, bf16[64,128]{1,0:T(8,128)(2,1)} %pv_ref.1, bf16[80,128]{1,0:T(8,128)(2,1)} %kw_ref.1, bf16[80,128]{1,0:T(8,128)(2,1)} %vw_ref.1, ...), custom_call_target="tpu_custom_call" | custom-call | tf_op jit(solution)/shard_map/attention_back/pallas_call | solution.py:350
  85.2 0.0 copy-start.2
  85.2 0.0 copy-start.1
  85.2 1.7 %copy.20 = bf16[128,1024]{1,0:T(8,128)(2,1)} copy(bf16[128,1024]{1,0:T(8,128)(2,1)} %get-tuple-element.8) | data formatting | bytes 524288
  86.9 0.0 copy-done.2
  86.9 0.0 copy-start
  86.9 0.6 copy.21
  87.5 0.0 copy-done.1
  87.5 0.6 copy.22
  88.1 0.0 copy-done
  88.1 0.6 copy.23
Async XLA Ops:
  85.2 1.7 %copy-start.2 = (bf16[128,128]{1,0:T(8,128)(2,1)S(1)}, bf16[128,128]{1,0:T(8,128)(2,1)}, u32[]{:S(2)}) copy-start(bf16[128,128]{1,0:T(8,128)(2,1)} %get-tuple-element.9) | copy-start | bytes 98308
  85.2 2.3 %copy-start.1 = (bf16[128,128]{1,0:T(8,128)(2,1)S(1)}, bf16[128,128]{1,0:T(8,128)(2,1)}, u32[]{:S(2)}) copy-start(bf16[128,128]{1,0:T(8,128)(2,1)} %get-tuple-element.10) | copy-start | bytes 98308
  86.9 1.2 %copy-start = (bf16[64,640]{1,0:T(8,128)(2,1)S(1)}, bf16[64,640]{1,0:T(8,128)(2,1)}, u32[]{:S(2)}) copy-start(bf16[64,640]{1,0:T(8,128)(2,1)} %get-tuple-element.11) | copy-start | bytes 245764

commit v3 on v2

--- a/solution.py
+++ b/solution.py
@@ -19,8 +19,8 @@
 MESH = pl.DeviceIdType.MESH
 BF, F32 = jnp.bfloat16, jnp.float32
 Z_RANKS = (0, 1, 7, 2, 6, 3, 5, 4)
-Z_FAR = Z_RANKS[:0:-1]
-X_ORDER = (2, 1, 3)
+Z_GROUPS = ((0, 1), (1, 2), (3, 2), (5, 2), (7, 1))
+GO_RIGHT = (0, 1, 4)
 Y_ORDER = (4, 3, 5, 2, 6, 1, 7)
 Y_NEAR = (1, 7, 2, 6, 3, 5, 4)
 
@@ -58,11 +58,10 @@
     pk_ref, pv_ref, kw_ref, vw_ref, q_ref, rk_ref, rv_ref, g_ref, lse_ref, delta_ref, prompt_in, len_in,
     dq_ref, drk_ref, drv_ref, out_ref,
     prompt_ref, len_ref, kv, wst, wbuf, q, g, rk, rv, lse, delta, lse_t, delta_t,
-    own, sib, table, table_s, snd1, rcv1, snd2, rcv2, rcv3,
+    own, sib, table, table_s, snd0, rcv0, snd1, rcv1, snd2, rcv2, rcv3,
     load_sem, table_sem,
-    kz_s, kz_r, kx_s, kx_r, kc_s, kc_r,
-    w0_s, w0_r, wx_s, wx_r, wz_s, wz_r, wc_s, wc_r,
-    rc_s, rc_r, rx_s, rx_r, rz_s, rz_r, ry_s, ry_r,
+    kv_s, kv_r, w0_s, w0_r, wg_s, wg_r,
+    rc_s, rc_r, rf_s, rf_r, rn_s, rn_r, rz_s, rz_r, ry_s, ry_r,
 ):
     me = lax.axis_index("dp")
     t = lax.axis_index("tensor")
@@ -123,72 +122,118 @@
         copy.start()
         sent.append(copy)
 
+    def gather(buf, s, r, ring):
+        def copy(n, src, dst, dev):
+            return remote(src, dst, s.at[n], r.at[n], dev)
+
+        def over_z(i):
+            k = Z_RANKS[i]
+            if not ring:
+                return copy(i, buf.at[c, x, 0], buf.at[c, x, i], zp(k))
+            way = 1 if k <= 4 else -1
+            return copy(i, buf.at[c, x, Z_RANKS.index((k - way) % NZ)], buf.at[c, x, i], zp(way % NZ))
+
+        def part(xx, group):
+            first, count = Z_GROUPS[group]
+            return buf.at[c, xx, pl.ds(first, count)]
+
+        def near(group, way, came=False):
+            ref = part((x - way + NX) % NX if came else x, group)
+            return copy(8 + 2 * group + (way < 0), ref, ref, xp(way % NX))
+
+        def far(group, came=False):
+            way = 1 if group in GO_RIGHT else -1
+            ref = part((x - 2 + NX) % NX if came else (x - way + NX) % NX, group)
+            return copy(18 + group, ref, ref, xp(way % NX))
+
+        def cross(k, came=False):
+            ref = buf.at[1 - c if came else c, (x - k + NX) % NX]
+            return copy(23 + k, ref, ref, other)
+
+        for i in (1, 2) if ring else range(NZ - 1, 0, -1):
+            go(over_z(i))
+        for way in (1, -1):
+            go(near(0, way))
+        yield
+        for group in range(1, 5):
+            first, count = Z_GROUPS[group]
+            for i in range(first, first + count):
+                over_z(i).wait_recv()
+                if ring and i + 2 < NZ:
+                    go(over_z(i + 2))
+            for way in (1, -1):
+                go(near(group, way))
+            for way in (1, -1):
+                near(group - 1, way, True).wait_recv()
+            go(far(group - 1))
+            yield
+        go(cross(0))
+        for way in (1, -1):
+            near(4, way, True).wait_recv()
+        go(far(4))
+        go(cross(1))
+        go(cross(3))
+        yield
+        for group in range(5):
+            far(group, True).wait_recv()
+        go(cross(2))
+        yield
+        for k in range(NX):
+            cross(k, True).wait_recv()
+        yield
+
     wt_c, wt_z, wt_x = (me // 4) % 2, t, (me % 4 + 1) % NX
 
-    def wz(i):
-        return remote(wbuf.at[c, x, 0], wbuf.at[c, x, i], wz_s.at[i], wz_r.at[i], zp(Z_RANKS[i]))
-
-    def wx(k):
-        return remote(wbuf.at[c, x], wbuf.at[c, x], wx_s.at[k], wx_r.at[k], xp(k))
-
-    def wx_in(k):
-        dst = wbuf.at[c, (x - k + NX) % NX]
-        return remote(dst, dst, wx_s.at[k], wx_r.at[k], xp(k))
-
-    def wc(k):
-        group = wbuf.at[c, (x - k + NX) % NX]
-        return remote(group, group, wc_s.at[k], wc_r.at[k], other)
-
-    def wc_in(k):
-        group = wbuf.at[1 - c, (x - k + NX) % NX]
-        return remote(group, group, wc_s.at[k], wc_r.at[k], other)
-
-    def weights(step):
-        if step == 0:
-            go(remote(wst, wbuf.at[wt_c, wt_x, 0], w0_s, w0_r, w_to))
-        elif step == 1:
-            remote(wst, wbuf.at[c, x, 0], w0_s, w0_r, w_to).wait_recv()
-            for i in range(NZ - 1, 0, -1):
-                go(wz(i))
-        elif step == 2:
-            for i in range(1, NZ):
-                wz(i).wait_recv()
-            for k in X_ORDER:
-                go(wx(k))
-            go(wc(0))
-        elif step == 3:
-            for k in (1, 3, 2):
-                wx_in(k).wait_recv()
-                go(wc(k))
-        else:
-            for k in range(NX):
-                wc_in(k).wait_recv()
-
-    def kz(i):
-        return remote(kv.at[c, x, 0], kv.at[c, x, i], kz_s.at[i], kz_r.at[i], zp(Z_RANKS[i]))
-
-    def half_of(cc, xx, half):
-        return kv.at[cc, xx, pl.ds(4 * half, 4)]
-
-    def kx(k, half):
-        group = half_of(c, x, half)
-        return remote(group, group, kx_s.at[k, half], kx_r.at[k, half], xp(k))
-
-    def kx_in(k, half):
-        group = half_of(c, (x - k + NX) % NX, half)
-        return remote(group, group, kx_s.at[k, half], kx_r.at[k, half], xp(k))
-
-    def kc(k, half):
-        group = half_of(c, (x - k + NX) % NX, half)
-        return remote(group, group, kc_s.at[k, half], kc_r.at[k, half], other)
-
-    def kc_in(k, half):
-        group = half_of(1 - c, (x - k + NX) % NX, half)
-        return remote(group, group, kc_s.at[k, half], kc_r.at[k, half], other)
-
-    for i in range(NZ - 1, 0, -1):
-        go(kz(i))
-    weights(0)
+    def gather_weights():
+        def copy(n, src, dst, dev):
+            return remote(src, dst, wg_s.at[n], wg_r.at[n], dev)
+
+        def over_x(k, came=False):
+            ref = wbuf.at[c, 0, (x - k + NX) % NX if came else x]
+            return copy(k, ref, ref, xp(k))
+
+        def hop(i, way):
+            before = Z_RANKS.index((Z_RANKS[i] - way) % NZ)
+            if i < NZ - 1:
+                return copy(4 + i, wbuf.at[c, before], wbuf.at[c, i], zp(way % NZ))
+            part = pl.ds(0 if way == 1 else 2, 2)
+            return copy(11 + (way == 1), wbuf.at[c, before, part], wbuf.at[c, i, part], zp(way % NZ))
+
+        def cross(i, came=False):
+            ref = wbuf.at[1 - c if came else c, i]
+            return copy(13 + i, ref, ref, other)
+
+        go(remote(wst, wbuf.at[wt_c, 0, wt_x], w0_s, w0_r, w_to))
+        yield
+        remote(wst, wbuf.at[c, 0, x], w0_s, w0_r, w_to).wait_recv()
+        for k in (2, 1, 3):
+            go(over_x(k))
+        yield
+        for k in (1, 3, 2):
+            over_x(k, True).wait_recv()
+        go(hop(1, 1))
+        go(hop(2, -1))
+        go(cross(0))
+        yield
+        for i, way in ((1, 1), (2, -1), (3, 1), (4, -1), (5, 1), (6, -1)):
+            hop(i, way).wait_recv()
+            go(hop(min(i + 2, NZ - 1), way))
+            go(cross(i))
+            if way == -1:
+                yield
+        for way in (1, -1):
+            hop(NZ - 1, way).wait_recv()
+        go(cross(NZ - 1))
+        yield
+        for i in range(NZ):
+            cross(i, True).wait_recv()
+        yield
+
+    prompts = gather(kv, kv_s, kv_r, True)
+    weights = gather_weights()
+
+    next(prompts)
+    next(weights, None)
 
     for copy in loads[4:]:
         copy.wait()
@@ -210,20 +255,15 @@
     lse_t[...] = spread_rows(lse[...])
     delta_t[...] = spread_rows(delta[...])
 
-    for half in range(2):
-        for i in range(max(4 * half, 1), 4 * half + 4):
-            kz(i).wait_recv()
-        for k in X_ORDER:
-            go(kx(k, half))
-        go(kc(0, half))
-    weights(1)
-    for half in range(2):
-        for k in (1, 3, 2):
-            kx_in(k, half).wait_recv()
-            go(kc(k, half))
-    for half in range(2):
-        for k in range(NX):
-            kc_in(k, half).wait_recv()
+    next(prompts)
+    next(prompts)
+    next(prompts)
+    next(weights, None)
+    next(prompts)
+    next(prompts)
+    next(prompts)
+    next(weights, None)
+    next(prompts)
 
     key_row = lax.broadcasted_iota(jnp.int32, (2 * LP + 16, HD), 0)
     column = lax.broadcasted_iota(jnp.int32, (2 * LP + 16, HD), 1)
@@ -266,8 +306,8 @@
         one_pair(2 * i)
         one_pair(2 * i + 1)
         go(rc(i))
-        if i == 1:
-            weights(2)
+        for _ in range((0, 1, 0, 1)[i]):
+            next(weights, None)
 
     table_copy.wait()
     for i in range(4):
@@ -277,8 +317,13 @@
         rows = slice(LP * part, LP * (part + 1))
         return own[table_s[0, j], rows].astype(F32) + sib[table_s[1, j], rows].astype(F32)
 
-    def rx(k, part):
-        return remote(snd1.at[part, k - 1], rcv1.at[part, k - 1], rx_s.at[part, k - 1], rx_r.at[part, k - 1], xp(k))
+    def rf(way, part):
+        n = 0 if way == 1 else 1
+        return remote(snd0.at[part, n], rcv0.at[part, n], rf_s.at[part, n], rf_r.at[part, n], xp(way % NX))
+
+    def rn(way, part):
+        n = 0 if way == 1 else 1
+        return remote(snd1.at[part, n], rcv1.at[part, n], rn_s.at[part, n], rn_r.at[part, n], xp(way % NX))
 
     def rz(i, part):
         return remote(snd2.at[part, i], rcv2.at[part, i], rz_s.at[part, i], rz_r.at[part, i], zp(Z_RANKS[i]))
@@ -291,25 +336,39 @@
         return (z + Z_RANKS[i]) % NZ
 
     for part in range(2):
-        for k in X_ORDER:
-            for i in range(NZ):
-                snd1[part, k - 1, i] = both_cores(at((x + k) % NX, ahead(i), c), part).astype(BF)
-            go(rx(k, part))
+        for way in (1, -1):
+            first = 0 if way == 1 else 4
+            for i in range(4):
+                j = at((x + 2) % NX, ahead(first + i), c)
+                snd0[part, first // 4, i] = both_cores(j, part).astype(BF)
+            go(rf(way, part))
+    for part in range(2):
+        for way in (1, -1):
+            n = 0 if way == 1 else 1
+            for i in [i for i in range(NZ) if i // 4 != n] + [i for i in range(NZ) if i // 4 == n]:
+                if i == 4 * n:
+                    rf(way, part).wait_recv()
+                total = both_cores(at((x + way) % NX, ahead(i), c), part)
+                if i // 4 == n:
+                    total = total + rcv0[part, n, i - 4 * n].astype(F32)
+                snd1[part, n, i] = total.astype(BF)
+            go(rn(way, part))
+    next(weights, None)
 
     mine = [None, None]
     for part in range(2):
-        for k in (1, 3, 2):
-            rx(k, part).wait_recv()
+        for way in (1, -1):
+            rn(way, part).wait_recv()
         for i in range(NZ - 1, -1, -1):
             total = both_cores(at(x, ahead(i), c), part)
-            for k in range(NX - 1):
-                total = total + rcv1[part, k, i].astype(F32)
+            for n in range(2):
+                total = total + rcv1[part, n, i].astype(F32)
             if i:
                 snd2[part, i] = total.astype(BF)
                 go(rz(i, part))
             else:
                 mine[part] = total
-    weights(3)
+    next(weights, None)
     for part in range(2):
         for i in range(1, NZ):
             rz(i, part).wait_recv()
@@ -317,7 +376,7 @@
         rcv3[0, LP * part : LP * (part + 1)] = (mine[part] * SCALE if part == 0 else mine[part]).astype(BF)
         for k in Y_ORDER:
             go(ry(k, part))
-    weights(4)
+    next(weights, None)
 
     def project(k):
         head = (t - k + NY) % NY
@@ -327,7 +386,7 @@
         weights = []
         for cc in range(NC):
             for j in range(4):
-                block = wbuf[cc, (j + 1) % NX, place]
+                block = wbuf[cc, place, (j + 1) % NX]
                 weights.append(jnp.concatenate([block[:WROWS], block[WROWS:]], axis=1))
         return dot_nt(both, jnp.concatenate(weights, axis=0))
 
@@ -362,7 +421,7 @@
             pltpu.SMEM((SLOTS,), jnp.int32),
             pltpu.VMEM((NC, NX, NZ, 2 * LP, HD), BF),
             pltpu.VMEM((2 * WROWS, HD), BF),
-            pltpu.VMEM((NC, NX, NZ, 2 * WROWS, HD), BF),
+            pltpu.VMEM((NC, NZ, NX, 2 * WROWS, HD), BF),
             pltpu.VMEM((rows, HEADS * HD), BF),
             pltpu.VMEM((rows, HEADS * HD), BF),
             pltpu.VMEM((rows, HD), BF),
@@ -375,16 +434,18 @@
             pltpu.VMEM((SLOTS + 1, 2 * LP, HD), BF),
             pltpu.VMEM((8, HD), jnp.int32),
             pltpu.SMEM((8, HD), jnp.int32),
-            pltpu.VMEM((2, NX - 1, NZ, LP, HD), BF),
-            pltpu.VMEM((2, NX - 1, NZ, LP, HD), BF),
+            pltpu.VMEM((2, 2, NZ // 2, LP, HD), BF),
+            pltpu.VMEM((2, 2, NZ // 2, LP, HD), BF),
+            pltpu.VMEM((2, 2, NZ, LP, HD), BF),
+            pltpu.VMEM((2, 2, NZ, LP, HD), BF),
             pltpu.VMEM((2, NZ, LP, HD), BF),
             pltpu.VMEM((2, NZ, LP, HD), BF),
             pltpu.VMEM((NY, 2 * LP, HD), BF),
             dma((12,)),
             dma,
-            dma((NZ,)), dma((NZ,)), dma((NX, 2)), dma((NX, 2)), dma((NX, 2)), dma((NX, 2)),
-            dma, dma, dma((NX,)), dma((NX,)), dma((NZ,)), dma((NZ,)), dma((NX,)), dma((NX,)),
-            dma((4,)), dma((4,)), dma((2, NX - 1)), dma((2, NX - 1)), dma((2, NZ)), dma((2, NZ)), dma((2, NY)), dma((2, NY)),
+            dma((27,)), dma((27,)), dma, dma, dma((27,)), dma((27,)),
+            dma((4,)), dma((4,)), dma((2, 2)), dma((2, 2)), dma((2, 2)), dma((2, 2)),
+            dma((2, NZ)), dma((2, NZ)), dma((2, NY)), dma((2, NY)),
         ],
         compiler_params=pltpu.CompilerParams(
             collective_id=0, has_side_effects=True, vmem_limit_bytes=62 << 20

time: 89 us -> 75.9 us (0.85)
  Pallas kernels: 84.6 us -> 71.4 us
    pallas_call x1, Pallas kernels: 84.6 us -> 71.4 us  [body(): pl.pallas_call(kernel, out_shape=(jax.ShapeDtypeStruct((rows, HEADS * HD)...]
where the time goes in v3:
time: 75.9 us; the launch traced here: 75.6 us
  Pallas kernels  71.4 us (94%)
  local copies, waits for them, and re-layouts  3.56 us (5%)
    pallas_call x1, Pallas kernels, body(): pl.pallas_call(kernel, out_shape=(jax.ShapeDtypeStruct((rows, HEADS * HD)...  71.4 us
    unnamed x10, local copies, waits for them, and re-layouts  3.56 us

profile of v3, /device:TPU:2, one launch (start us, length us, event | category | flops | bytes accessed | tf_op | source)
XLA Modules:
  0.0 75.6 jit_solution(1824006831923646707)
XLA Ops:
  0.6 71.4 %attention_back.1 = (bf16[128,1024]{1,0:T(8,128)(2,1)}, bf16[128,128]{1,0:T(8,128)(2,1)}, bf16[128,128]{1,0:T(8,128)(2,1)}, bf16[64,640]{1,0:T(8,128)(2,1)}) custom-call(bf16[64,128]{1,0:T(8,128)(2,1)} %pk_ref.1, bf16[64,128]{1,0:T(8,128)(2,1)} %pv_ref.1, bf16[80,128]{1,0:T(8,128)(2,1)} %kw_ref.1, bf16[80,128]{1,0:T(8,128)(2,1)} %vw_ref.1, ...), custom_call_target="tpu_custom_call" | custom-call | tf_op jit(solution)/shard_map/attention_back/pallas_call | solution.py:409
  72.0 0.0 copy-start.2
  72.0 0.0 copy-start.1
  72.0 1.7 %copy.20 = bf16[128,1024]{1,0:T(8,128)(2,1)} copy(bf16[128,1024]{1,0:T(8,128)(2,1)} %get-tuple-element.8) | data formatting | bytes 524288
  73.7 0.0 copy-done.2
  73.7 0.0 copy-start
  73.7 0.6 copy.21
  74.3 0.0 copy-done.1
  74.3 0.6 copy.22
  75.0 0.0 copy-done
  75.0 0.6 copy.23
Async XLA Ops:
  72.0 1.7 %copy-start.2 = (bf16[128,128]{1,0:T(8,128)(2,1)S(1)}, bf16[128,128]{1,0:T(8,128)(2,1)}, u32[]{:S(2)}) copy-start(bf16[128,128]{1,0:T(8,128)(2,1)} %get-tuple-element.9) | copy-start | bytes 98308
  72.0 2.3 %copy-start.1 = (bf16[128,128]{1,0:T(8,128)(2,1)S(1)}, bf16[128,128]{1,0:T(8,128)(2,1)}, u32[]{:S(2)}) copy-start(bf16[128,128]{1,0:T(8,128)(2,1)} %get-tuple-element.10) | copy-start | bytes 98308
  73.7 1.2 %copy-start = (bf16[64,640]{1,0:T(8,128)(2,1)S(1)}, bf16[64,640]{1,0:T(8,128)(2,1)}, u32[]{:S(2)}) copy-start(bf16[64,640]{1,0:T(8,128)(2,1)} %get-tuple-element.11) | copy-start | bytes 245764

commit v4 on v3

--- a/solution.py
+++ b/solution.py
@@ -56,8 +56,8 @@
 
 def kernel(
     pk_ref, pv_ref, kw_ref, vw_ref, q_ref, rk_ref, rv_ref, g_ref, lse_ref, delta_ref, prompt_in, len_in,
-    dq_ref, drk_ref, drv_ref, out_ref,
-    prompt_ref, len_ref, kv, wst, wbuf, q, g, rk, rv, lse, delta, lse_t, delta_t,
+    dq_out, drk_out, drv_out, input_out,
+    dq_ref, drk_ref, drv_ref, out_ref, out_sem, prompt_ref, len_ref, kv, wst, wbuf, q, g, rk, rv, lse, delta, lse_t, delta_t,
     own, sib, table, table_s, snd0, rcv0, snd1, rcv1, snd2, rcv2, rcv3,
     load_sem, table_sem,
     kv_s, kv_r, w0_s, w0_r, wg_s, wg_r,
@@ -149,6 +149,10 @@
         def cross(k, came=False):
             ref = buf.at[1 - c if came else c, (x - k + NX) % NX]
             return copy(23 + k, ref, ref, other)
+
+        def cross_far(half, came=False):
+            ref = buf.at[1 - c if came else c, (x - 2 + NX) % NX, pl.ds(5 * half, 5 - 2 * half)]
+            return copy(25 if half else 27, ref, ref, other)
 
         for i in (1, 2) if ring else range(NZ - 1, 0, -1):
             go(over_z(i))
@@ -174,12 +178,15 @@
         go(cross(1))
         go(cross(3))
         yield
-        for group in range(5):
-            far(group, True).wait_recv()
-        go(cross(2))
-        yield
-        for k in range(NX):
+        for half in range(2):
+            for group in ((0, 1, 2), (3, 4))[half]:
+                far(group, True).wait_recv()
+            go(cross_far(half))
+        yield
+        for k in (0, 1, 3):
             cross(k, True).wait_recv()
+        for half in range(2):
+            cross_far(half, True).wait_recv()
         yield
 
     wt_c, wt_z, wt_x = (me // 4) % 2, t, (me % 4 + 1) % NX
@@ -235,6 +242,14 @@
     next(prompts)
     next(weights, None)
 
+    next(prompts)
+    next(prompts)
+    next(weights, None)
+    next(prompts)
+    next(prompts)
+    next(prompts)
+    next(weights, None)
+    next(prompts)
     for copy in loads[4:]:
         copy.wait()
 
@@ -256,14 +271,7 @@
     delta_t[...] = spread_rows(delta[...])
 
     next(prompts)
-    next(prompts)
-    next(prompts)
-    next(weights, None)
-    next(prompts)
-    next(prompts)
-    next(prompts)
-    next(weights, None)
-    next(prompts)
+    next(weights, None)
 
     key_row = lax.broadcasted_iota(jnp.int32, (2 * LP + 16, HD), 0)
     column = lax.broadcasted_iota(jnp.int32, (2 * LP + 16, HD), 1)
@@ -306,9 +314,17 @@
         one_pair(2 * i)
         one_pair(2 * i + 1)
         go(rc(i))
-        for _ in range((0, 1, 0, 1)[i]):
+        for _ in range((0, 0, 0, 1)[i]):
             next(weights, None)
 
+    stores = [
+        pltpu.make_async_copy(a, b, out_sem.at[i])
+        for i, (a, b) in enumerate(
+            ((dq_ref, dq_out), (drk_ref, drk_out), (drv_ref, drv_out), (out_ref, input_out))
+        )
+    ]
+    for copy in stores[:3]:
+        copy.start()
     table_copy.wait()
     for i in range(4):
         rc(i).wait_recv()
@@ -396,27 +412,40 @@
             ry(k, part).wait_recv()
         acc = acc + project(k)
     out_ref[...] = acc.astype(BF)
-
+    stores[3].start()
     for copy in sent:
         copy.wait_send()
+    for copy in stores:
+        copy.wait()
+
+
+def store(*refs):
+    arrays, outs, tiles, sem = refs[:4], refs[4:8], refs[8:12], refs[12]
+    loads = [pltpu.make_async_copy(a, b, sem.at[0, i]) for i, (a, b) in enumerate(zip(arrays, tiles))]
+    stores = [pltpu.make_async_copy(a, b, sem.at[1, i]) for i, (a, b) in enumerate(zip(tiles, outs))]
+    for copy in loads:
+        copy.start()
+    for load, copy in zip(loads, stores):
+        load.wait()
+        copy.start()
+    for copy in stores:
+        copy.wait()
 
 
 def body(*args):
-    vmem = pl.BlockSpec(memory_space=pltpu.VMEM)
     hbm = pl.BlockSpec(memory_space=pl.ANY)
     rows = SLOTS * LR
     dma = pltpu.SemaphoreType.DMA
-    return pl.pallas_call(
+    shapes = ((rows, HEADS * HD), (rows, HD), (rows, HD), (LP, 8 * WROWS))
+    results = tuple(jax.ShapeDtypeStruct(shape, BF) for shape in shapes)
+    grads = pl.pallas_call(
         kernel,
-        out_shape=(
-            jax.ShapeDtypeStruct((rows, HEADS * HD), BF),
-            jax.ShapeDtypeStruct((rows, HD), BF),
-            jax.ShapeDtypeStruct((rows, HD), BF),
-            jax.ShapeDtypeStruct((LP, 8 * WROWS), BF),
-        ),
+        out_shape=results,
         in_specs=[hbm] * 12,
-        out_specs=(vmem,) * 4,
+        out_specs=(hbm,) * 4,
         scratch_shapes=[
+            *(pltpu.VMEM(shape, BF) for shape in shapes),
+            dma((4,)),
             pltpu.SMEM((64 * SLOTS,), jnp.int32),
             pltpu.SMEM((SLOTS,), jnp.int32),
             pltpu.VMEM((NC, NX, NZ, 2 * LP, HD), BF),
@@ -443,7 +472,7 @@
             pltpu.VMEM((NY, 2 * LP, HD), BF),
             dma((12,)),
             dma,
-            dma((27,)), dma((27,)), dma, dma, dma((27,)), dma((27,)),
+            dma((28,)), dma((28,)), dma, dma, dma((28,)), dma((28,)),
             dma((4,)), dma((4,)), dma((2, 2)), dma((2, 2)), dma((2, 2)), dma((2, 2)),
             dma((2, NZ)), dma((2, NZ)), dma((2, NY)), dma((2, NY)),
         ],
@@ -452,6 +481,15 @@
         ),
         name="attention_back",
     )(*args)
+    return pl.pallas_call(
+        store,
+        out_shape=results,
+        in_specs=[hbm] * 4,
+        out_specs=(hbm,) * 4,
+        scratch_shapes=[*(pltpu.VMEM(shape, BF) for shape in shapes), dma((2, 4))],
+        compiler_params=pltpu.CompilerParams(vmem_limit_bytes=62 << 20),
+        name="store",
+    )(*grads)
 
 
 def solution(mesh):

time: 75.9 us -> 72.7 us (0.958)
  local copies, waits for them, and re-layouts: 3.56 us -> 0 us
    unnamed x10 -> x0, local copies, waits for them, and re-layouts: 3.56 us -> none
    pallas_call x1 -> x2, Pallas kernels: 71.4 us -> 71.9 us  [the longest x1 70.1 us: body(): pl.pallas_call(kernel, out_shape=results, in_specs=[hbm] * 12, out_specs=...]
where the time goes in v4:
time: 72.7 us; the launch traced here: 72.5 us
  Pallas kernels  71.9 us (99%)
    pallas_call x1, Pallas kernels, body(): pl.pallas_call(kernel, out_shape=results, in_specs=[hbm] * 12, out_specs=...  70.1 us
    pallas_call x1, Pallas kernels, body(): pl.pallas_call(store, out_shape=results, in_specs=[hbm] * 4, out_specs=(h...  1.76 us

profile of v4, /device:TPU:2, one launch (start us, length us, event | category | flops | bytes accessed | tf_op | source)
XLA Modules:
  0.0 72.5 jit_solution(3490273280361128077)
XLA Ops:
  0.6 70.1 %attention_back.1 = (bf16[128,1024]{1,0:T(8,128)(2,1)}, bf16[128,128]{1,0:T(8,128)(2,1)}, bf16[128,128]{1,0:T(8,128)(2,1)}, bf16[64,640]{1,0:T(8,128)(2,1)}) custom-call(bf16[64,128]{1,0:T(8,128)(2,1)} %pk_ref.1, bf16[64,128]{1,0:T(8,128)(2,1)} %pv_ref.1, bf16[80,128]{1,0:T(8,128)(2,1)} %kw_ref.1, bf16[80,128]{1,0:T(8,128)(2,1)} %vw_ref.1, ...), custom_call_target="tpu_custom_call" | custom-call | tf_op jit(solution)/shard_map/attention_back/pallas_call | solution.py:441
  70.8 1.8 %store.1 = (bf16[128,1024]{1,0:T(8,128)(2,1)}, bf16[128,128]{1,0:T(8,128)(2,1)}, bf16[128,128]{1,0:T(8,128)(2,1)}, bf16[64,640]{1,0:T(8,128)(2,1)}) custom-call(bf16[128,1024]{1,0:T(8,128)(2,1)} %get-tuple-element.8.refs_0_, bf16[128,128]{1,0:T(8,128)(2,1)} %get-tuple-element.9.refs_1_, bf16[128,128]{1,0:T(8,128)(2,1)} %get-tuple-element.10.refs_2_, ...), custom_call_target="tpu_custom_call" | custom-call | tf_op jit(solution)/shard_map/store/pallas_call | solution.py:484

commit v5 on v4

--- a/solution.py
+++ b/solution.py
@@ -15,6 +15,8 @@
 PAIRS = SLOTS // 2
 NX, NZ, NC, NY = 4, 8, 2, 8
 WROWS = 80
+PARTS = 4
+PART = 2 * LP // PARTS
 SCALE = 1.0 / math.sqrt(HD)
 MESH = pl.DeviceIdType.MESH
 BF, F32 = jnp.bfloat16, jnp.float32
@@ -243,13 +245,14 @@
     next(weights, None)
 
     next(prompts)
-    next(prompts)
-    next(weights, None)
-    next(prompts)
-    next(prompts)
-    next(prompts)
-    next(weights, None)
-    next(prompts)
+    next(weights, None)
+    next(prompts)
+    next(prompts)
+    next(weights, None)
+    next(prompts)
+    next(prompts)
+    next(prompts)
+    next(weights, None)
     for copy in loads[4:]:
         copy.wait()
 
@@ -271,7 +274,6 @@
     delta_t[...] = spread_rows(delta[...])
 
     next(prompts)
-    next(weights, None)
 
     key_row = lax.broadcasted_iota(jnp.int32, (2 * LP + 16, HD), 0)
     column = lax.broadcasted_iota(jnp.int32, (2 * LP + 16, HD), 1)
@@ -330,7 +332,7 @@
         rc(i).wait_recv()
 
     def both_cores(j, part):
-        rows = slice(LP * part, LP * (part + 1))
+        rows = slice(PART * part, PART * (part + 1))
         return own[table_s[0, j], rows].astype(F32) + sib[table_s[1, j], rows].astype(F32)
 
     def rf(way, part):
@@ -345,20 +347,20 @@
         return remote(snd2.at[part, i], rcv2.at[part, i], rz_s.at[part, i], rz_r.at[part, i], zp(Z_RANKS[i]))
 
     def ry(k, part):
-        rows = pl.ds(LP * part, LP)
+        rows = pl.ds(PART * part, PART)
         return remote(rcv3.at[0, rows], rcv3.at[k, rows], ry_s.at[part, k], ry_r.at[part, k], yp(k))
 
     def ahead(i):
         return (z + Z_RANKS[i]) % NZ
 
-    for part in range(2):
+    for part in range(PARTS):
         for way in (1, -1):
             first = 0 if way == 1 else 4
             for i in range(4):
                 j = at((x + 2) % NX, ahead(first + i), c)
                 snd0[part, first // 4, i] = both_cores(j, part).astype(BF)
             go(rf(way, part))
-    for part in range(2):
+    for part in range(PARTS):
         for way in (1, -1):
             n = 0 if way == 1 else 1
             for i in [i for i in range(NZ) if i // 4 != n] + [i for i in range(NZ) if i // 4 == n]:
@@ -371,8 +373,8 @@
             go(rn(way, part))
     next(weights, None)
 
-    mine = [None, None]
-    for part in range(2):
+    mine = [None] * PARTS
+    for part in range(PARTS):
         for way in (1, -1):
             rn(way, part).wait_recv()
         for i in range(NZ - 1, -1, -1):
@@ -385,11 +387,11 @@
             else:
                 mine[part] = total
     next(weights, None)
-    for part in range(2):
+    for part in range(PARTS):
         for i in range(1, NZ):
             rz(i, part).wait_recv()
             mine[part] = mine[part] + rcv2[part, i].astype(F32)
-        rcv3[0, LP * part : LP * (part + 1)] = (mine[part] * SCALE if part == 0 else mine[part]).astype(BF)
+        rcv3[0, PART * part : PART * (part + 1)] = (mine[part] * SCALE if PART * part < LP else mine[part]).astype(BF)
         for k in Y_ORDER:
             go(ry(k, part))
     next(weights, None)
@@ -408,7 +410,7 @@
 
     acc = project(0)
     for k in Y_NEAR:
-        for part in range(2):
+        for part in range(PARTS):
             ry(k, part).wait_recv()
         acc = acc + project(k)
     out_ref[...] = acc.astype(BF)
@@ -463,18 +465,18 @@
             pltpu.VMEM((SLOTS + 1, 2 * LP, HD), BF),
             pltpu.VMEM((8, HD), jnp.int32),
             pltpu.SMEM((8, HD), jnp.int32),
-            pltpu.VMEM((2, 2, NZ // 2, LP, HD), BF),
-            pltpu.VMEM((2, 2, NZ // 2, LP, HD), BF),
-            pltpu.VMEM((2, 2, NZ, LP, HD), BF),
-            pltpu.VMEM((2, 2, NZ, LP, HD), BF),
-            pltpu.VMEM((2, NZ, LP, HD), BF),
-            pltpu.VMEM((2, NZ, LP, HD), BF),
+            pltpu.VMEM((PARTS, 2, NZ // 2, PART, HD), BF),
+            pltpu.VMEM((PARTS, 2, NZ // 2, PART, HD), BF),
+            pltpu.VMEM((PARTS, 2, NZ, PART, HD), BF),
+            pltpu.VMEM((PARTS, 2, NZ, PART, HD), BF),
+            pltpu.VMEM((PARTS, NZ, PART, HD), BF),
+            pltpu.VMEM((PARTS, NZ, PART, HD), BF),
             pltpu.VMEM((NY, 2 * LP, HD), BF),
             dma((12,)),
             dma,
             dma((28,)), dma((28,)), dma, dma, dma((28,)), dma((28,)),
-            dma((4,)), dma((4,)), dma((2, 2)), dma((2, 2)), dma((2, 2)), dma((2, 2)),
-            dma((2, NZ)), dma((2, NZ)), dma((2, NY)), dma((2, NY)),
+            dma((4,)), dma((4,)), dma((PARTS, 2)), dma((PARTS, 2)), dma((PARTS, 2)), dma((PARTS, 2)),
+            dma((PARTS, NZ)), dma((PARTS, NZ)), dma((PARTS, NY)), dma((PARTS, NY)),
         ],
         compiler_params=pltpu.CompilerParams(
             collective_id=0, has_side_effects=True, vmem_limit_bytes=62 << 20

time: 72.7 us -> 70.2 us (0.966)
  Pallas kernels: 71.9 us -> 69.4 us
    pallas_call x1, Pallas kernels: 70.1 us -> 67.6 us  [body(): pl.pallas_call(kernel, out_shape=results, in_specs=[hbm] * 12, out_specs=...]
where the time goes in v5:
time: 70.2 us; the launch traced here: 70 us
  Pallas kernels  69.4 us (99%)
    pallas_call x1, Pallas kernels, body(): pl.pallas_call(kernel, out_shape=results, in_specs=[hbm] * 12, out_specs=...  67.6 us
    pallas_call x1, Pallas kernels, body(): pl.pallas_call(store, out_shape=results, in_specs=[hbm] * 4, out_specs=(h...  1.76 us

profile of v5, /device:TPU:2, one launch (start us, length us, event | category | flops | bytes accessed | tf_op | source)
XLA Modules:
  0.0 70.0 jit_solution(16229731001537835126)
XLA Ops:
  0.6 67.6 %attention_back.1 = (bf16[128,1024]{1,0:T(8,128)(2,1)}, bf16[128,128]{1,0:T(8,128)(2,1)}, bf16[128,128]{1,0:T(8,128)(2,1)}, bf16[64,640]{1,0:T(8,128)(2,1)}) custom-call(bf16[64,128]{1,0:T(8,128)(2,1)} %pk_ref.1, bf16[64,128]{1,0:T(8,128)(2,1)} %pv_ref.1, bf16[80,128]{1,0:T(8,128)(2,1)} %kw_ref.1, bf16[80,128]{1,0:T(8,128)(2,1)} %vw_ref.1, ...), custom_call_target="tpu_custom_call" | custom-call | tf_op jit(solution)/shard_map/attention_back/pallas_call | solution.py:443
  68.3 1.8 %store.1 = (bf16[128,1024]{1,0:T(8,128)(2,1)}, bf16[128,128]{1,0:T(8,128)(2,1)}, bf16[128,128]{1,0:T(8,128)(2,1)}, bf16[64,640]{1,0:T(8,128)(2,1)}) custom-call(bf16[128,1024]{1,0:T(8,128)(2,1)} %get-tuple-element.8.refs_0_, bf16[128,128]{1,0:T(8,128)(2,1)} %get-tuple-element.9.refs_1_, bf16[128,128]{1,0:T(8,128)(2,1)} %get-tuple-element.10.refs_2_, ...), custom_call_target="tpu_custom_call" | custom-call | tf_op jit(solution)/shard_map/store/pallas_call | solution.py:486

commit v6 on v5

--- a/solution.py
+++ b/solution.py
@@ -316,8 +316,6 @@
         one_pair(2 * i)
         one_pair(2 * i + 1)
         go(rc(i))
-        for _ in range((0, 0, 0, 1)[i]):
-            next(weights, None)
 
     stores = [
         pltpu.make_async_copy(a, b, out_sem.at[i])
@@ -360,6 +358,7 @@
                 j = at((x + 2) % NX, ahead(first + i), c)
                 snd0[part, first // 4, i] = both_cores(j, part).astype(BF)
             go(rf(way, part))
+    next(weights, None)
     for part in range(PARTS):
         for way in (1, -1):
             n = 0 if way == 1 else 1

time: 70.2 us -> 69.7 us (level)
  no operation moved by 1% of the time
where the time goes in v6:
time: 69.7 us; the launch traced here: 69.5 us
  Pallas kernels  68.8 us (99%)
    pallas_call x1, Pallas kernels, body(): pl.pallas_call(kernel, out_shape=results, in_specs=[hbm] * 12, out_specs=...  67.1 us
    pallas_call x1, Pallas kernels, body(): pl.pallas_call(store, out_shape=results, in_specs=[hbm] * 4, out_specs=(h...  1.76 us

profile of v6, /device:TPU:2, one launch (start us, length us, event | category | flops | bytes accessed | tf_op | source)
XLA Modules:
  0.0 69.5 jit_solution(14889550898620804655)
XLA Ops:
  0.6 67.1 %attention_back.1 = (bf16[128,1024]{1,0:T(8,128)(2,1)}, bf16[128,128]{1,0:T(8,128)(2,1)}, bf16[128,128]{1,0:T(8,128)(2,1)}, bf16[64,640]{1,0:T(8,128)(2,1)}) custom-call(bf16[64,128]{1,0:T(8,128)(2,1)} %pk_ref.1, bf16[64,128]{1,0:T(8,128)(2,1)} %pv_ref.1, bf16[80,128]{1,0:T(8,128)(2,1)} %kw_ref.1, bf16[80,128]{1,0:T(8,128)(2,1)} %vw_ref.1, ...), custom_call_target="tpu_custom_call" | custom-call | tf_op jit(solution)/shard_map/attention_back/pallas_call | solution.py:442
  67.7 1.8 %store.1 = (bf16[128,1024]{1,0:T(8,128)(2,1)}, bf16[128,128]{1,0:T(8,128)(2,1)}, bf16[128,128]{1,0:T(8,128)(2,1)}, bf16[64,640]{1,0:T(8,128)(2,1)}) custom-call(bf16[128,1024]{1,0:T(8,128)(2,1)} %get-tuple-element.8.refs_0_, bf16[128,128]{1,0:T(8,128)(2,1)} %get-tuple-element.9.refs_1_, bf16[128,128]{1,0:T(8,128)(2,1)} %get-tuple-element.10.refs_2_, ...), custom_call_target="tpu_custom_call" | custom-call | tf_op jit(solution)/shard_map/store/pallas_call | solution.py:485

commit v7 on v6

--- a/solution.py
+++ b/solution.py
@@ -15,7 +15,7 @@
 PAIRS = SLOTS // 2
 NX, NZ, NC, NY = 4, 8, 2, 8
 WROWS = 80
-PARTS = 4
+PARTS = 8
 PART = 2 * LP // PARTS
 SCALE = 1.0 / math.sqrt(HD)
 MESH = pl.DeviceIdType.MESH

time: 69.7 us -> 71.1 us (1.020)
  the two profiles are of different devices: /device:TPU:2 before, /device:TPU:8 now
where the time goes in v7:
time: 71.1 us; the launch traced here: 70.9 us
  Pallas kernels  70.3 us (99%)
    pallas_call x1, Pallas kernels, body(): pl.pallas_call(kernel, out_shape=results, in_specs=[hbm] * 12, out_specs=...  68.5 us
    pallas_call x1, Pallas kernels, body(): pl.pallas_call(store, out_shape=results, in_specs=[hbm] * 4, out_specs=(h...  1.76 us

profile of v7, /device:TPU:8, one launch (start us, length us, event | category | flops | bytes accessed | tf_op | source)
XLA Modules:
  0.0 70.9 jit_solution(4170666343063837547)
XLA Ops:
  0.6 68.5 %attention_back.1 = (bf16[128,1024]{1,0:T(8,128)(2,1)}, bf16[128,128]{1,0:T(8,128)(2,1)}, bf16[128,128]{1,0:T(8,128)(2,1)}, bf16[64,640]{1,0:T(8,128)(2,1)}) custom-call(bf16[64,128]{1,0:T(8,128)(2,1)} %pk_ref.1, bf16[64,128]{1,0:T(8,128)(2,1)} %pv_ref.1, bf16[80,128]{1,0:T(8,128)(2,1)} %kw_ref.1, bf16[80,128]{1,0:T(8,128)(2,1)} %vw_ref.1, ...), custom_call_target="tpu_custom_call" | custom-call | tf_op jit(solution)/shard_map/attention_back/pallas_call | solution.py:442
  69.2 1.8 %store.1 = (bf16[128,1024]{1,0:T(8,128)(2,1)}, bf16[128,128]{1,0:T(8,128)(2,1)}, bf16[128,128]{1,0:T(8,128)(2,1)}, bf16[64,640]{1,0:T(8,128)(2,1)}) custom-call(bf16[128,1024]{1,0:T(8,128)(2,1)} %get-tuple-element.8.refs_0_, bf16[128,128]{1,0:T(8,128)(2,1)} %get-tuple-element.9.refs_1_, bf16[128,128]{1,0:T(8,128)(2,1)} %get-tuple-element.10.refs_2_, ...), custom_call_target="tpu_custom_call" | custom-call | tf_op jit(solution)/shard_map/store/pallas_call | solution.py:485
